TPU v7x, 256 devices: a whole 4x4x8 slice. The times are simulated.
256 devices in a mesh: level: 8 (over x, core), panel: 32 (over y, z).
Axes of the slice: x: 4, y: 4, z: 8, core: 2. Of those that a mesh axis runs over, the one named last changes fastest.
Arguments:
- contrib: bfloat16 [8, 8192, 8192], P('level', None, 'panel'), may hold values from -6 to 6
- pattern: int32 [8, 64, 64], P('level'), may hold values 0 or 1
- pivot_inverse: bfloat16 [8, 2, 128, 128], replicated, may hold values from -0.005859375 to 0.005859375
Outputs:
- schur: bfloat16 [8192, 8192], P('level', 'panel')
All inputs are finite; a program needn't handle non-finite values. No bound on the sum of `pattern` on one device may be relied on, other than what follows from the above.
Results may differ from a plain program's by a relative error of at most 0.012.
Values may be sent and summed in bfloat16 or wider, within the bound.
A program may use at most 128 MiB of HBM per device.

v0:
```python
import jax
import jax.numpy as jnp
from jax import lax
from jax.sharding import PartitionSpec as P

PANEL = 128
SEP = 2


def from_partner(shard, axis, bit):
    return lax.ppermute(shard, axis, [(i, i ^ 1 << bit) for i in range(lax.axis_size(axis))])


def broadcast(value, axis, source):
    kept = jnp.where(lax.axis_index(axis) == source, value, 0).astype(value.dtype)
    return lax.psum(kept, axis)


def weights_of(mat, inverse, row_start, pivot_idx, mat_panel):
    pivot_rows = lax.slice_in_dim(mat, row_start, row_start + PANEL, axis=0).astype(jnp.bfloat16)
    weights = jnp.dot(inverse, pivot_rows, preferred_element_type=jnp.float32)
    return jnp.where((mat_panel > pivot_idx)[None, :], weights, 0.0).astype(jnp.bfloat16)


def update(mat, pivot_col, weights):
    return mat - jnp.dot(pivot_col, weights, preferred_element_type=jnp.float32)


def body(contrib, pattern, pivot_inverse):
    front_rows = contrib.shape[1]
    local_width = contrib.shape[2]
    npanels = local_width // PANEL
    blocks = front_rows // PANEL
    level_count = lax.axis_size("level")
    levels = level_count.bit_length() - 1
    level_at = lax.axis_index("level")
    panel_at = lax.axis_index("panel")
    block_rows = front_rows // level_count
    col_mask = lax.dynamic_slice_in_dim(pattern[0], panel_at * npanels, npanels, 1)
    masked = (
        contrib[0].reshape(blocks, PANEL, npanels, PANEL)
        * col_mask.astype(jnp.bfloat16)[:, None, :, None]
    )
    carried = masked.reshape(front_rows, local_width)
    row_panel = jnp.arange(front_rows) // PANEL
    col_panel = panel_at * npanels + jnp.arange(local_width) // PANEL
    for tree_level in range(levels):
        partner = from_partner(carried, "level", tree_level)
        front_mat = carried.astype(jnp.float32) + partner.astype(jnp.float32)
        sep_first = tree_level * SEP
        sep_end = sep_first + SEP
        is_sep = (col_panel >= sep_first) & (col_panel < sep_end)
        front_mat = jnp.where(
            is_sep[None, :], front_mat.astype(jnp.bfloat16).astype(jnp.float32), front_mat
        )
        subcube = level_at >> tree_level + 1
        leader = (2 * subcube + 1) * 2**tree_level - 1
        factors = lax.dynamic_index_in_dim(pivot_inverse, leader, 0, keepdims=False)
        for panel_step in range(SEP):
            pivot_idx = sep_first + panel_step
            offset = pivot_idx % npanels * PANEL
            column = lax.slice_in_dim(front_mat, offset, offset + PANEL, axis=1)
            pivot_col = jnp.where((row_panel > pivot_idx)[:, None], column, 0.0).astype(
                jnp.bfloat16
            )
            pivot_col = broadcast(pivot_col, "panel", pivot_idx // npanels)
            weights = weights_of(
                front_mat, factors[panel_step], pivot_idx * PANEL, pivot_idx, col_panel
            )
            front_mat = update(front_mat, pivot_col, weights)
        keep_rows = row_panel >= sep_end
        keep_cols = col_panel >= sep_end
        carried = jnp.where(keep_rows[:, None] & keep_cols[None, :], front_mat, 0.0).astype(
            jnp.bfloat16
        )
    return lax.dynamic_slice_in_dim(carried, level_at * block_rows, block_rows, 0)


def solution(mesh):
    in_specs = (P("level", None, "panel"), P("level", None, None), P())
    out_specs = P("level", "panel")
    return jax.shard_map(body, mesh=mesh, in_specs=in_specs, out_specs=out_specs, check_vma=False)
```

profile of v0, /device:TPU:2, one launch (start us, length us, event | category | flops | bytes accessed | tf_op | source)
XLA Modules:
  0.0 1226.9 jit_solution(16238122300774386113)
XLA Ops:
  12.4 7.5 collective-permute-done
  19.9 4.4 convert_select_fusion.2
  27.5 5.0 fusion.13
  32.7 157.3 %all-reduce.7.cloned.1.call-done = bf16[8192,128]{1,0:T(8,128)(2,1)} async-done(((bf16[8192,128]{1,0:T(8,128)(2,1)}), bf16[8192,128]{1,0:T(8,128)(2,1)}) %all-reduce.7.cloned.1.call-update) | async-done | bytes 2097168 | tf_op jit(solution)/shard_map/psum | solution.py:16
  190.0 8.7 convolution_subtract_fusion.4
  198.7 7.0 fusion.14
  205.9 151.2 %all-reduce.9.cloned.1.call-done = bf16[8192,128]{1,0:T(8,128)(2,1)} async-done(((bf16[8192,128]{1,0:T(8,128)(2,1)}), bf16[8192,128]{1,0:T(8,128)(2,1)}) %all-reduce.9.cloned.1.call-update) | async-done | bytes 2097168 | tf_op jit(solution)/shard_map/psum | solution.py:16
  357.1 6.4 fusion.2
  364.0 87.5 %collective-permute-done.1 = bf16[8192,256]{1,0:T(8,128)(2,1)} collective-permute-done((bf16[8192,256]{1,0:T(8,128)(2,1)}, bf16[8192,256]{1,0:T(8,128)(2,1)}, u32[]{:S(2)}, u32[]{:S(2)}) %collective-permute-start.1) | collective-permute-done | bytes 4194336 | tf_op jit(solution)/shard_map/ppermute | solution.py:11
  451.6 4.4 convert_select_fusion.1
  459.2 5.0 fusion.15
  464.6 151.7 %all-reduce.11.cloned.1.call-done = bf16[8192,128]{1,0:T(8,128)(2,1)} async-done(((bf16[8192,128]{1,0:T(8,128)(2,1)}), bf16[8192,128]{1,0:T(8,128)(2,1)}) %all-reduce.11.cloned.1.call-update) | async-done | bytes 2097168 | tf_op jit(solution)/shard_map/psum | solution.py:16
  616.2 8.7 convolution_subtract_fusion.2
  625.0 7.0 fusion.16
  632.1 151.2 %all-reduce.13.cloned.1.call-done = bf16[8192,128]{1,0:T(8,128)(2,1)} async-done(((bf16[8192,128]{1,0:T(8,128)(2,1)}), bf16[8192,128]{1,0:T(8,128)(2,1)}) %all-reduce.13.cloned.1.call-update) | async-done | bytes 2097168 | tf_op jit(solution)/shard_map/psum | solution.py:16
  783.3 6.4 fusion.3
  791.8 87.5 %collective-permute-done.2 = bf16[8192,256]{1,0:T(8,128)(2,1)} collective-permute-done((bf16[8192,256]{1,0:T(8,128)(2,1)}, bf16[8192,256]{1,0:T(8,128)(2,1)}, u32[]{:S(2)}, u32[]{:S(2)}) %collective-permute-start.2) | collective-permute-done | bytes 4194336 | tf_op jit(solution)/shard_map/ppermute | solution.py:11
  879.3 4.4 convert_select_fusion
  887.0 5.0 fusion.17
  892.1 151.9 %all-reduce.15.cloned.1.call-done = bf16[8192,128]{1,0:T(8,128)(2,1)} async-done(((bf16[8192,128]{1,0:T(8,128)(2,1)}), bf16[8192,128]{1,0:T(8,128)(2,1)}) %all-reduce.15.cloned.1.call-update) | async-done | bytes 2097168 | tf_op jit(solution)/shard_map/psum | solution.py:16
  1044.0 8.7 convolution_subtract_fusion
  1052.7 7.0 fusion.18
  1059.8 151.3 %all-reduce.17.cloned.1.call-done = bf16[8192,128]{1,0:T(8,128)(2,1)} async-done(((bf16[8192,128]{1,0:T(8,128)(2,1)}), bf16[8192,128]{1,0:T(8,128)(2,1)}) %all-reduce.17.cloned.1.call-update) | async-done | bytes 2097168 | tf_op jit(solution)/shard_map/psum | solution.py:16
  1211.1 6.2 fusion.25
  (50 shorter events, 21.5 us)
Async XLA Ops:
  6.5 183.5 %copy-start = (bf16[8,2,128,128]{3,2,1,0:T(8,128)(2,1)S(1)}, bf16[8,2,128,128]{3,2,1,0:T(8,128)(2,1)}, u32[]{:S(2)}) copy-start(bf16[8,2,128,128]{3,2,1,0:T(8,128)(2,1)} %param.5) | copy-start | bytes 1572868
  6.5 183.5 %all-reduce.7.cloned.1.call-start = ((), (), s32[]{:S(2)}) async-start(), calls=%async_computation | async-start | bytes 4194304 | tf_op jit(solution)/shard_map/psum | solution.py:16
  7.6 2.2 copy-start.4
  12.4 7.5 collective-permute-start
  24.3 3.2 copy-start.2
  32.6 324.5 %all-reduce.9.cloned.1.call-start = ((), (), s32[]{:S(2)}) async-start(), calls=%async_computation.1 | async-start | bytes 4194304 | tf_op jit(solution)/shard_map/psum | solution.py:16
  205.8 410.5 %all-reduce.11.cloned.1.call-start = ((), (), s32[]{:S(2)}) async-start(), calls=%async_computation.2 | async-start | bytes 4194304 | tf_op jit(solution)/shard_map/psum | solution.py:16
  363.5 88.1 %collective-permute-start.1 = (bf16[8192,256]{1,0:T(8,128)(2,1)}, bf16[8192,256]{1,0:T(8,128)(2,1)}, u32[]{:S(2)}, u32[]{:S(2)}) collective-permute-start(bf16[8192,256]{1,0:T(8,128)(2,1)} %fusion.2), channel_id=1, source_target_pairs={{0,64},{32,96},{64,0},{96,32},{128,192},{160,224},{192,128},{224,1... | collective-permute-start | bytes 12582920 | tf_op jit(solution)/shard_map/ppermute | solution.py:11
  456.0 3.2 copy-start.3
  464.3 318.9 %all-reduce.13.cloned.1.call-start = ((), (), s32[]{:S(2)}) async-start(), calls=%async_computation.3 | async-start | bytes 4194304 | tf_op jit(solution)/shard_map/psum | solution.py:16
  632.0 412.0 %all-reduce.15.cloned.1.call-start = ((), (), s32[]{:S(2)}) async-start(), calls=%async_computation.4 | async-start | bytes 4194304 | tf_op jit(solution)/shard_map/psum | solution.py:16
  789.7 89.6 %collective-permute-start.2 = (bf16[8192,256]{1,0:T(8,128)(2,1)}, bf16[8192,256]{1,0:T(8,128)(2,1)}, u32[]{:S(2)}, u32[]{:S(2)}) collective-permute-start(bf16[8192,256]{1,0:T(8,128)(2,1)} %fusion.3), channel_id=1, source_target_pairs={{0,128},{32,160},{64,192},{96,224},{128,0},{160,32},{192,64},{224,... | collective-permute-start | bytes 12582920 | tf_op jit(solution)/shard_map/ppermute | solution.py:11
  883.7 3.2 copy-start.1
  892.0 319.1 %all-reduce.17.cloned.1.call-start = ((), (), s32[]{:S(2)}) async-start(), calls=%async_computation.5 | async-start | bytes 4194304 | tf_op jit(solution)/shard_map/psum | solution.py:16
Sparse Core Ops, SparseCore 0:
  32.7 157.2 all-reduce.6
  205.9 151.1 all-reduce.8
  464.4 151.7 all-reduce.10
  632.1 151.0 all-reduce.12
  892.2 151.8 all-reduce.14
  1059.9 151.1 all-reduce.16
where the time goes:
time: 1230 us
  waiting for transfers between devices  1100 us (89%)
  other arithmetic  55.6 us (5%)
  matrix products  45.2 us (4%)
  between operations  13.7 us (1%)
    psum x6, waiting for transfers between devices, broadcast(): return lax.psum(kept, axis)  915 us
    ppermute x3, waiting for transfers between devices, from_partner(): lax.ppermute(shard, axis, [(i, i ^ 1 << bit) for i in range(lax.axis_size...  183 us
    dot_general x6, matrix products, update(): return mat - jnp.dot(pivot_col, weights, preferred_element_type=jnp.float32)  45.2 us
    select_n x6, other arithmetic, broadcast(): jnp.where(lax.axis_index(axis) == source, value, 0).astype(value.dtype)  36.2 us
  transfers between devices with their start and end apart: 9, of which 9 were waited for; matrix products, arithmetic and copies ran while one was open for 0% of the time, Pallas kernels for 0%

commit v1 on v0

v1 whole, which is shorter than its diff:
```python
import functools

import jax
import jax.numpy as jnp
from jax import lax
from jax.experimental import pallas as pl
from jax.experimental.pallas import tpu as pltpu
from jax.sharding import PartitionSpec as P

MESH = pl.DeviceIdType.MESH
PANEL = 128
W = 256
SEP_END = 3 * W
NX, NC = 4, 2
ROWS = 1024
KC, KL = 8, 16
FLOWS = (
    (0, "A", 1),
    (0, "B", 1),
    (0, "A", -1),
    (0, "B", -1),
    (1, "A", 1),
    (1, "A", -1),
    (2, "B", 1),
    (2, "B", -1),
)
X_ORDER = (0, 1, 3, 2)
BF, F32 = jnp.bfloat16, jnp.float32


def dot(a, b):
    return jnp.dot(a, b, preferred_element_type=F32)


def pivots(sep, rows, inverse):
    first = dot(inverse[0], rows[:PANEL]).astype(BF)
    second_rows = (rows[PANEL:].astype(F32) - dot(sep[PANEL:, :PANEL], first)).astype(BF)
    second = dot(inverse[1], second_rows).astype(BF)
    between = dot(inverse[0], sep[:PANEL, PANEL:]).astype(BF)
    return jnp.concatenate([(first.astype(F32) - dot(between, second)).astype(BF), second], 0)


def kernel(
    ny, nz,
    pattern, contrib, inv, out,
    sent, own, xin, fin, trx, l0, l1, l2, c0, c1, c2, q, vx, acc,
    core_send, core_recv, trx_send, trx_recv, xin_send, xin_recv,
    fc_send, fc_recv, fl_send, fl_recv, q_send, q_recv,
):
    level, panel = lax.axis_index("level"), lax.axis_index("panel")
    x, c = level // NC, level % NC
    y, z = panel // nz, panel % nz
    other = (x * NC + 1 - c, panel)
    to_x = [(lax.rem(x + d, NX) * NC + c, panel) for d in (1, 3, 2)]
    to_y = {1: (level, lax.rem(y + 1, ny) * nz + z), -1: (level, lax.rem(y + ny - 1, ny) * nz + z)}
    to_z = {1: (level, y * nz + lax.rem(z + 1, nz)), -1: (level, y * nz + lax.rem(z + nz - 1, nz))}

    barrier = pltpu.get_barrier_semaphore()
    partners = [other] + to_x + [to_y[1], to_y[-1], to_z[1], to_z[-1]]
    for partner in partners:
        pl.semaphore_signal(barrier, inc=1, device_id=partner, device_id_type=MESH)
    pl.semaphore_wait(barrier, len(partners))

    def remote(src, dst, send, recv, device):
        return pltpu.make_async_remote_copy(
            src_ref=src, dst_ref=dst, send_sem=send, recv_sem=recv, device_id=device, device_id_type=MESH
        )

    lane = lax.broadcasted_iota(jnp.int32, (1, W), 1)

    def mask_block(target, j, parity):
        def step(i, carry):
            row = (j * NC + parity) * (ROWS // PANEL) + i
            left = pattern[row, panel * 2].astype(F32)
            right = pattern[row, panel * 2 + 1].astype(F32)
            factor = jnp.where(lane < PANEL, left, right)
            block = contrib[pl.ds(pl.multiple_of(row * PANEL, PANEL), PANEL), :].astype(F32) * factor
            target[j, pl.ds(pl.multiple_of(i * PANEL, PANEL), PANEL), :] = block.astype(BF)
            return carry

        lax.fori_loop(0, ROWS // PANEL, step, 0)

    core_copies = [remote(sent.at[j], fin.at[j], core_send.at[j], core_recv.at[j], other) for j in range(NX)]
    for j in range(NX):
        mask_block(sent, j, 1 - c)
        core_copies[j].start()
    for j in range(NX):
        mask_block(own, j, c)

    def add_block(j):
        core_copies[j].wait_recv()
        own[j] = (own[j].astype(F32) + fin[j].astype(F32)).astype(BF)

    add_block(0)
    trx_copies = [
        remote(own.at[0, pl.ds(0, SEP_END)], trx.at[x], trx_send.at[i], trx_recv.at[x], to_x[i]) for i in range(3)
    ]

    @pl.when(c == 0)
    def _():
        for copy in trx_copies:
            copy.start()

    for j in range(1, NX):
        add_block(j)
    xin_copies = []
    for i, d in enumerate((1, 3, 2)):
        there = lax.rem(x + d, NX)
        copy = remote(own.at[there], xin.at[x], xin_send.at[i], xin_recv.at[x], to_x[i])
        copy.start()
        xin_copies.append(copy)
    xin[x] = own[x]

    def wait_xin(there):
        remote(own.at[0], xin.at[there], xin_send.at[0], xin_recv.at[there], to_x[0]).wait_recv()

    @pl.when(c == 0)
    def _():
        trx[x] = own[0, :SEP_END]
        for d in (1, 3, 2):
            there = lax.rem(x + d, NX)
            remote(
                own.at[0, pl.ds(0, SEP_END)], trx.at[there], trx_send.at[0], trx_recv.at[there], to_x[0]
            ).wait_recv()

        @pl.when(panel == 0)
        def _():
            for i in range(NX):
                c0[i * SEP_END:(i + 1) * SEP_END] = trx[i]

        @pl.when(panel == 1)
        def _():
            for i in range(NX):
                c1[i * W:(i + 1) * W] = trx[i, :W]
            for g in range(2):
                total = trx[2 * g, W:].astype(F32) + trx[2 * g + 1, W:].astype(F32)
                c1[NX * W + g * 2 * W:NX * W + (g + 1) * 2 * W] = total.astype(BF)

        @pl.when(panel == 2)
        def _():
            for i in range(NX):
                c2[i * W:(i + 1) * W] = trx[i, :W]
            for g in range(2):
                total = trx[2 * g, W:2 * W].astype(F32) + trx[2 * g + 1, W:2 * W].astype(F32)
                c2[(NX + g) * W:(NX + g + 1) * W] = total.astype(BF)
            total = sum(trx[i, 2 * W:].astype(F32) for i in range(NX))
            c2[6 * W:] = total.astype(BF)

    def place(slab, kind, sign):
        if sign == 1:
            dy, dz = y, lax.rem(z - slab + nz, nz)
        else:
            dy, dz = lax.rem(ny - y, ny), lax.rem(slab - z + nz, nz)
        if kind == "A":
            depth = jnp.where(dy == 0, dz, jnp.where(dz >= 1, dz + dy, nz + dy))
            go_z = ((dy == 0) & (dz < nz - 1)) | ((dy >= 1) & (dz == nz - 1))
            go_y = (dz >= 1) & (dy < ny - 1)
        else:
            depth = jnp.where(dz == 0, dy, jnp.where(dy >= 1, dy + dz, ny + dz))
            go_y = ((dz == 0) & (dy < ny - 1)) | ((dz >= 1) & (dy == ny - 1))
            go_z = (dy >= 1) & (dz < nz - 1)
        return depth, go_y, go_z

    places = [place(*flow) for flow in FLOWS]
    part = {0: 0, 1: 0, 2: 0}
    tree = []
    for slab, _, _ in FLOWS:
        tree.append(part[slab])
        part[slab] += 1

    def top_item(f, k):
        slab, t = FLOWS[f][0], tree[f]
        if slab == 0:
            n = SEP_END // 4 // (KC // NX)
            row = (k // (KC // NX)) * SEP_END + t * (SEP_END // 4) + lax.rem(k, KC // NX) * n
            return c0.at[pl.ds(pl.multiple_of(row, 16), n)]
        ref, rows = (c1, 8 * W) if slab == 1 else (c2, 7 * W)
        n = rows // 2 // KC
        return ref.at[pl.ds(pl.multiple_of(t * (rows // 2) + k * n, 16), n)]

    def long_item(f, k):
        slab, t = FLOWS[f][0], tree[f]
        if slab == 0:
            per = KL // NX
            n = ROWS // 4 // per
            j = k // per
            there = lax.rem(x + jnp.where(j < 2, j, 5 - j), NX)
            row = there * ROWS + t * (ROWS // 4) + lax.rem(k, per) * n
            return l0.at[pl.ds(pl.multiple_of(row, 16), n)]
        if slab == 1:
            per = KL // 2
            n = ROWS // 2 // per
            row = (k // per) * ROWS + t * (ROWS // 2) + lax.rem(k, per) * n
            return l1.at[pl.ds(pl.multiple_of(row, 16), n)]
        n = ROWS // 2 // KL
        return l2.at[pl.ds(pl.multiple_of(t * (ROWS // 2) + k * n, 16), n)]

    def handle(f, k, item, send, recv):
        slab, _, sign = FLOWS[f]
        depth, go_y, go_z = places[f]
        ref = item(f, k)
        half = lax.rem(k, 2)

        @pl.when(depth > 0)
        def _():
            remote(ref, ref, send.at[f, 0, half], recv.at[f, k], to_z[sign]).wait_recv()

        for i, (go, device) in enumerate(((go_z, to_z[sign]), (go_y, to_y[sign]))):
            @pl.when(go)
            def _():
                copy = remote(ref, ref, send.at[f, i, half], recv.at[f, k], device)

                @pl.when(k >= 2)
                def _():
                    copy.wait_send()

                copy.start()

    def step(tau, carry):
        k_long = tau - KC

        @pl.when((panel == 0) & (k_long >= 0) & (k_long < KL) & (lax.rem(k_long + KL, KL // NX) == 0))
        def _():
            j = k_long // (KL // NX)
            there = lax.rem(x + jnp.where(j < 2, j, 5 - j), NX)

            @pl.when(j > 0)
            def _():
                wait_xin(there)

            l0[pl.ds(pl.multiple_of(there * ROWS, ROWS), ROWS), :] = xin[there]

        @pl.when(((panel == 1) | (panel == 2)) & (k_long == 0))
        def _():
            for d in (1, 3, 2):
                wait_xin(lax.rem(x + d, NX))

            @pl.when(panel == 1)
            def _():
                for g in range(2):
                    total = xin[2 * g].astype(F32) + xin[2 * g + 1].astype(F32)
                    l1[g * ROWS:(g + 1) * ROWS] = total.astype(BF)

            @pl.when(panel == 2)
            def _():
                l2[...] = sum(xin[i].astype(F32) for i in range(NX)).astype(BF)

        for f in range(len(FLOWS)):
            k = tau - places[f][0]

            @pl.when((c == 0) & (k >= 0) & (k < KC))
            def _():
                handle(f, k, top_item, fc_send, fc_recv)

            @pl.when((k >= KC) & (k < KC + KL))
            def _():
                handle(f, k - KC, long_item, fl_send, fl_recv)

        return carry

    lax.fori_loop(jnp.where(c == 0, 0, KC), KC + KL + ny + nz - 1, step, 0)

    for copy in core_copies + xin_copies:
        copy.wait_send()

    @pl.when(c == 0)
    def _():
        for copy in trx_copies:
            copy.wait_send()

    def drain(item, send, recv, count):
        for f, (slab, kind, sign) in enumerate(FLOWS):
            _, go_y, go_z = places[f]
            for i, (go, device) in enumerate(((go_z, to_z[sign]), (go_y, to_y[sign]))):
                @pl.when(go)
                def _():
                    for k in (count - 2, count - 1):
                        ref = item(f, k)
                        remote(ref, ref, send.at[f, i, k % 2], recv.at[f, k], device).wait_send()

    @pl.when(c == 0)
    def _():
        drain(top_item, fc_send, fc_recv, KC)

    drain(long_item, fl_send, fl_recv, KL)

    @pl.when(panel > 2)
    def _():
        for d in (1, 3, 2):
            wait_xin(lax.rem(x + d, NX))

    q_copy = remote(q, q, q_send, q_recv, other)

    @pl.when(c == 0)
    def _():
        for g in range(2):
            acc[g, :, :W] = c1[(4 + 2 * g) * W:(6 + 2 * g) * W].astype(F32)
            acc[g, :W, W:2 * W] = c2[(4 + g) * W:(5 + g) * W].astype(F32)
            acc[g, :W, 2 * W:] = trx[2 * g, W:2 * W].astype(F32) + trx[2 * g + 1, W:2 * W].astype(F32)
            acc[g, W:, W:] = jnp.zeros((W, 2 * W), F32)
            for i in (2 * g, 2 * g + 1):
                rows = jnp.concatenate(
                    [c1[i * W:(i + 1) * W], c2[i * W:(i + 1) * W], trx[i, :W]], axis=1
                )
                vx[i] = pivots(c0[i * SEP_END:i * SEP_END + W], rows, [inv[2 * i, 0], inv[2 * i, 1]])
                acc[g] -= dot(c0[i * SEP_END + W:(i + 1) * SEP_END], vx[i])
        last = [c2[6 * W:].astype(F32), sum(trx[i, 2 * W:].astype(F32) for i in range(NX))]
        last = jnp.concatenate(last, axis=1)
        vg = []
        for g in range(2):
            columns = acc[g, :, :W].astype(BF)
            vg.append(pivots(columns[:W], acc[g, :W, W:].astype(BF), [inv[4 * g + 1, 0], inv[4 * g + 1, 1]]))
            last = last + acc[g, W:, W:] - dot(columns[W:], vg[g])
        last = last.astype(BF)
        vh = pivots(last[:, :W], last[:, W:], [inv[3, 0], inv[3, 1]])
        q[6 * W:] = vh
        for g in range(2):
            qb = (vg[g][:, W:].astype(F32) - dot(vg[g][:, :W], vh)).astype(BF)
            q[(4 + g) * W:(5 + g) * W] = qb
            for i in (2 * g, 2 * g + 1):
                qa = vx[i, :, 2 * W:].astype(F32) - dot(vx[i, :, W:2 * W], vh) - dot(vx[i, :, :W], qb)
                q[i * W:(i + 1) * W] = qa.astype(BF)
        q_copy.start()
        q_copy.wait_send()

    @pl.when(c == 1)
    def _():
        q_copy.wait_recv()

    def finish(b, carry):
        n = 256
        here = pl.ds(pl.multiple_of(b * n, n), n)
        total = sum(xin[i, here].astype(F32) for i in range(NX))
        for i in range(7):
            if i < 4:
                block = l0[pl.ds(pl.multiple_of(i * ROWS + b * n, n), n), :]
            elif i < 6:
                block = l1[pl.ds(pl.multiple_of((i - 4) * ROWS + b * n, n), n), :]
            else:
                block = l2[here]
            total = total - dot(block, q[i * W:(i + 1) * W])
        kept = (panel > 2) & ((level > 0) | (b * n >= SEP_END))
        out[here, :] = jnp.where(kept, total, 0.0).astype(BF)
        return carry

    lax.fori_loop(0, ROWS // 256, finish, 0)


def solution(mesh):
    ny, nz = (4, 8) if mesh.shape["panel"] == 32 else (2, mesh.shape["panel"] // 2)

    def body(contrib, pattern, pivot_inverse):
        vmem = pl.BlockSpec(memory_space=pltpu.VMEM)
        dma = pltpu.SemaphoreType.DMA
        nf = len(FLOWS)
        return pl.pallas_call(
            functools.partial(kernel, ny, nz),
            out_shape=jax.ShapeDtypeStruct((ROWS, W), BF),
            in_specs=[pl.BlockSpec(memory_space=pltpu.SMEM), vmem, vmem],
            out_specs=vmem,
            scratch_shapes=[
                pltpu.VMEM((NX, ROWS, W), BF),
                pltpu.VMEM((NX, ROWS, W), BF),
                pltpu.VMEM((NX, ROWS, W), BF),
                pltpu.VMEM((NX, ROWS, W), BF),
                pltpu.VMEM((NX, SEP_END, W), BF),
                pltpu.VMEM((4 * ROWS, W), BF),
                pltpu.VMEM((2 * ROWS, W), BF),
                pltpu.VMEM((ROWS, W), BF),
                pltpu.VMEM((NX * SEP_END, W), BF),
                pltpu.VMEM((8 * W, W), BF),
                pltpu.VMEM((7 * W, W), BF),
                pltpu.VMEM((7 * W, W), BF),
                pltpu.VMEM((NX, W, 3 * W), BF),
                pltpu.VMEM((2, 2 * W, 3 * W), F32),
                dma((NX,)), dma((NX,)), dma((3,)), dma((NX,)), dma((3,)), dma((NX,)),
                dma((nf, 2, 2)), dma((nf, KC)), dma((nf, 2, 2)), dma((nf, KL)),
                dma, dma,
            ],
            compiler_params=pltpu.CompilerParams(
                collective_id=0, has_side_effects=True, vmem_limit_bytes=56 * 1024 * 1024
            ),
        )(pattern[0], contrib[0], pivot_inverse)

    in_specs = (P("level", None, "panel"), P("level", None, None), P())
    return jax.shard_map(body, mesh=mesh, in_specs=in_specs, out_specs=P("level", "panel"), check_vma=False)
```

time: 1230 us -> 156 us (0.13)
  the two profiles are of different devices: /device:TPU:2 before, /device:TPU:33 now
where the time goes in v1:
time: 156 us
  Pallas kernels  154 us (99%)
  local copies, waits for them, and re-layouts  1.87 us (1%)
    pallas_call x1, Pallas kernels, body(): pl.pallas_call(functools.partial(kernel, ny, nz), out_shape=jax.ShapeDtyp...  154 us

profile of v1, /device:TPU:33, one launch (start us, length us, event | category | flops | bytes accessed | tf_op | source)
XLA Modules:
  0.0 156.0 jit_solution(2554157620815646264)
XLA Ops:
  0.0 154.1 %shard_map.37 = bf16[1024,256]{1,0:T(8,128)(2,1)} custom-call(s32[64,64]{1,0:T(8,128)} %bitcast.3, bf16[8192,256]{1,0:T(8,128)(2,1)} %bitcast.2, bf16[8,2,128,128]{3,2,1,0:T(8,128)(2,1)} %inv.1), custom_call_target="tpu_custom_call" | custom-call | tf_op jit(solution)/shard_map/pallas_call | solution.py:356
  154.2 1.9 %copy.5 = bf16[1024,256]{1,0:T(8,128)(2,1)} copy(bf16[1024,256]{1,0:T(8,128)(2,1)} %shard_map.37) | data formatting | bytes 1048576

commit v2 on v1

v2 whole, which is shorter than its diff:
```python
import functools

import jax
import jax.numpy as jnp
import numpy as np
from jax import lax
from jax.experimental import pallas as pl
from jax.experimental.pallas import tpu as pltpu
from jax.sharding import PartitionSpec as P

MESH = pl.DeviceIdType.MESH
PANEL = 128
W = 256
SEP_END = 3 * W
NX, NC, NY, NZ = 4, 2, 4, 8
ROWS = 1024
BF, F32 = jnp.bfloat16, jnp.float32
TREES = (
    ((0xFE000082, 0x657D0001, 0x07440000, 0xE1240000), (0x55AA55AA, 0xC6113992, 0x38FEFE7C)),
    ((0x0080100C, 0x0A80000E, 0x3810387F, 0x028B0600), (0x55AA55AA, 0xE776E4CC, 0xF8FDFBF0)),
    ((0x007DCF01, 0x0000FE00, 0x40080700, 0x0440E100), (0x55AA55AA, 0xBB93C692, 0xFE7C387C)),
    ((0x00022070, 0x900200F0, 0x80A3C000, 0x181018FD), (0x55AA55AA, 0xCFDC4E66, 0x3E7FBF1E)),
)
DEPTH = 7
FLOWS = tuple((slab, tree) for slab in range(3) for tree in range(4))
KO, KC = 4, 8
KL = 4 * KO
SLOTS = KL + KC
KS = (KL, 8, 8)
TOPS = (SEP_END // KC, 64, 64)
TOP_ITEMS = (KC, 8, 7)
SKEW = 3


def dot(a, b):
    return jnp.dot(a, b, preferred_element_type=F32)


def bit(mask, at):
    return lax.shift_right_logical(jnp.int32(np.uint32(mask).astype(np.int32)), at) & 1


def pivots(sep, rows, inverse):
    first = dot(inverse[0], rows[:PANEL]).astype(BF)
    second_rows = (rows[PANEL:].astype(F32) - dot(sep[PANEL:, :PANEL], first)).astype(BF)
    second = dot(inverse[1], second_rows).astype(BF)
    between = dot(inverse[0], sep[:PANEL, PANEL:]).astype(BF)
    return jnp.concatenate([(first.astype(F32) - dot(between, second)).astype(BF), second], 0)


def kernel(
    pattern, contrib, inv_in, out,
    raw, inv, sent, own, xin, fin, trx, l0, l1, l2, c0, c1, c2, q, vx, acc,
    load, core_send, core_recv, trx_send, trx_recv, xin_send, xin_recv,
    fc_send, fc_recv, fl_send, fl_recv, q_send, q_recv,
):
    level, panel = lax.axis_index("level"), lax.axis_index("panel")
    x, c = level // NC, level % NC
    y, z = panel // NZ, panel % NZ
    other = (x * NC + 1 - c, panel)
    apart = (1, 3, 2)
    to_x = [(lax.rem(x + d, NX) * NC + c, panel) for d in apart]
    to = [
        (level, lax.rem(y + 1, NY) * NZ + z),
        (level, lax.rem(y + NY - 1, NY) * NZ + z),
        (level, y * NZ + lax.rem(z + 1, NZ)),
        (level, y * NZ + lax.rem(z + NZ - 1, NZ)),
    ]

    def remote(src, dst, send, recv, device):
        return pltpu.make_async_remote_copy(
            src_ref=src, dst_ref=dst, send_sem=send, recv_sem=recv, device_id=device, device_id_type=MESH
        )

    def load_block(i):
        rows = pl.ds(pl.multiple_of((NC * (i % NX) + jnp.where(i < NX, 1 - c, c)) * ROWS, ROWS), ROWS)
        return pltpu.make_async_copy(contrib.at[rows], raw.at[rows], load.at[i])

    loads = [load_block(i) for i in range(2 * NX)]
    for copy in loads:
        copy.start()
    inv_load = pltpu.make_async_copy(inv_in, inv, load.at[2 * NX])
    inv_load.start()

    barrier = pltpu.get_barrier_semaphore()
    partners = [other] + to_x + to
    for partner in partners:
        pl.semaphore_signal(barrier, inc=1, device_id=partner, device_id_type=MESH)
    pl.semaphore_wait(barrier, len(partners))

    lane = lax.broadcasted_iota(jnp.int32, (1, W), 1)

    def mask_block(target, j, parity):
        def step(i, carry):
            row = (j * NC + parity) * (ROWS // PANEL) + i
            left = pattern[row, panel * 2].astype(F32)
            right = pattern[row, panel * 2 + 1].astype(F32)
            factor = jnp.where(lane < PANEL, left, right)
            block = raw[pl.ds(pl.multiple_of(row * PANEL, PANEL), PANEL), :].astype(F32) * factor
            target[j, pl.ds(pl.multiple_of(i * PANEL, PANEL), PANEL), :] = block.astype(BF)
            return carry

        lax.fori_loop(0, ROWS // PANEL, step, 0)

    core_copies = [remote(sent.at[j], fin.at[j], core_send.at[j], core_recv.at[j], other) for j in range(NX)]

    def add_block(j):
        core_copies[j].wait_recv()
        own[j] = (own[j].astype(F32) + fin[j].astype(F32)).astype(BF)

    top_rows = own.at[0, pl.ds(0, SEP_END)]
    trx_copies = [remote(top_rows, trx.at[x], trx_send.at[i], trx_recv.at[x], to_x[i]) for i in range(3)]
    xin_copies = [
        remote(own.at[lax.rem(x + d, NX)], xin.at[x], xin_send.at[i], xin_recv.at[x], to_x[i])
        for i, d in enumerate(apart)
    ]

    def core_phase():
        for j in range(NX):
            loads[j].wait()
            mask_block(sent, j, 1 - c)
            core_copies[j].start()
        for j in range(NX):
            loads[NX + j].wait()
            mask_block(own, j, c)
        add_block(0)

    def x_phase():
        @pl.when(c == 0)
        def _():
            for copy in trx_copies:
                copy.start()

        for j in range(1, NX):
            add_block(j)
        for copy in xin_copies:
            copy.start()
        xin[x] = own[x]

    def wait_xin(there):
        remote(own.at[0], xin.at[there], xin_send.at[0], xin_recv.at[there], to_x[0]).wait_recv()

    def wait_trx():
        trx[x] = own[0, :SEP_END]
        for d in apart:
            there = lax.rem(x + d, NX)
            remote(top_rows, trx.at[there], trx_send.at[0], trx_recv.at[there], to_x[0]).wait_recv()

    def top_blocks():
        wait_trx()

        @pl.when(panel == 0)
        def _():
            for i in range(NX):
                c0[i * SEP_END:(i + 1) * SEP_END] = trx[i]

        @pl.when(panel == 1)
        def _():
            for i in range(NX):
                c1[i * W:(i + 1) * W] = trx[i, :W]
            for g in range(2):
                total = trx[2 * g, W:].astype(F32) + trx[2 * g + 1, W:].astype(F32)
                c1[NX * W + g * 2 * W:NX * W + (g + 1) * 2 * W] = total.astype(BF)

        @pl.when(panel == 2)
        def _():
            for i in range(NX):
                c2[i * W:(i + 1) * W] = trx[i, :W]
            for g in range(2):
                total = trx[2 * g, W:2 * W].astype(F32) + trx[2 * g + 1, W:2 * W].astype(F32)
                c2[(NX + g) * W:(NX + g + 1) * W] = total.astype(BF)
            c2[6 * W:] = sum(trx[i, 2 * W:].astype(F32) for i in range(NX)).astype(BF)

    places = []
    for slab, tree in FLOWS:
        at = y * NZ + lax.rem(z - slab + NZ, NZ)
        go, deep = TREES[tree]
        depth = bit(deep[0], at) + 2 * bit(deep[1], at) + 4 * bit(deep[2], at)
        places.append((depth, [bit(mask, at) == 1 for mask in go]))

    def top_item(f, k):
        slab, tree = FLOWS[f]
        n = TOPS[slab]
        if slab == 0:
            per = KC // NX
            row = (k // per) * SEP_END + tree * (SEP_END // 4) + lax.rem(k, per) * n
        else:
            row = (tree * TOP_ITEMS[slab] + k) * n
        return (c0, c1, c2)[slab].at[pl.ds(pl.multiple_of(row, 16), n)]

    def long_item(f, k):
        slab, tree = FLOWS[f]
        fronts = (4, 2, 1)[slab]
        per = KS[slab] // fronts
        n = ROWS // 4 // per
        j = k // per
        if slab == 0:
            j = lax.rem(x + jnp.where(j < 2, j, 5 - j), NX)
        row = j * ROWS + tree * (ROWS // 4) + lax.rem(k, per) * n
        return (l0, l1, l2)[slab].at[pl.ds(pl.multiple_of(row, 16), n)]

    def handle(f, k, item, send, recv):
        depth, go = places[f]
        ref = item(f, k)
        half = lax.rem(k, 2)

        @pl.when(depth > 0)
        def _():
            remote(ref, ref, send.at[f, 0, half], recv.at[f, k], to[0]).wait_recv()

        for i in range(4):
            @pl.when(go[i])
            def _():
                copy = remote(ref, ref, send.at[f, i, half], recv.at[f, k], to[i])

                @pl.when(k >= 2)
                def _():
                    copy.wait_send()

                copy.start()

    def prepare(slot):
        @pl.when((c == 0) & (panel < 3) & (slot == KO))
        def _():
            top_blocks()

        @pl.when((panel == 0) & (slot == 0))
        def _():
            l0[pl.ds(pl.multiple_of(x * ROWS, ROWS), ROWS), :] = own[x]

        @pl.when((panel == 0) & (slot >= KO + KC) & (slot < SLOTS) & (lax.rem(slot - KC, KO) == 0))
        def _():
            j = (slot - KC) // KO
            there = lax.rem(x + jnp.where(j < 2, j, 5 - j), NX)
            wait_xin(there)
            l0[pl.ds(pl.multiple_of(there * ROWS, ROWS), ROWS), :] = xin[there]

        @pl.when((panel == 1) & (slot == SLOTS - KS[1]))
        def _():
            for d in apart:
                wait_xin(lax.rem(x + d, NX))
            for g in range(2):
                total = xin[2 * g].astype(F32) + xin[2 * g + 1].astype(F32)
                l1[g * ROWS:(g + 1) * ROWS] = total.astype(BF)

        @pl.when((panel == 2) & (slot == SLOTS - KS[2]))
        def _():
            for d in apart:
                wait_xin(lax.rem(x + d, NX))
            l2[...] = sum(xin[i].astype(F32) for i in range(NX)).astype(BF)

    def step(tau, carry):
        prepare(tau)
        for f, (slab, _) in enumerate(FLOWS):
            slot = tau - SKEW * places[f][0]

            @pl.when((c == 0) & (slot >= KO) & (slot < KO + TOP_ITEMS[slab]))
            def _():
                handle(f, slot - KO, top_item, fc_send, fc_recv)

            if slab == 0:
                is_long = ((slot >= 0) & (slot < KO)) | ((slot >= KO + KC) & (slot < SLOTS))
                k = jnp.where(slot < KO, slot, slot - KC)
            else:
                is_long = (slot >= SLOTS - KS[slab]) & (slot < SLOTS)
                k = slot - (SLOTS - KS[slab])

            @pl.when(is_long)
            def _():
                handle(f, k, long_item, fl_send, fl_recv)

        return carry

    def flows():
        lax.fori_loop(0, SLOTS + SKEW * DEPTH, step, 0)

        @pl.when((c == 0) & (panel > 2))
        def _():
            wait_trx()

        @pl.when(panel > 2)
        def _():
            for d in apart:
                wait_xin(lax.rem(x + d, NX))

    def drain(item, send, recv, counts):
        for f, (slab, _) in enumerate(FLOWS):
            go = places[f][1]
            for i in range(4):
                @pl.when(go[i])
                def _():
                    for k in (counts[slab] - 2, counts[slab] - 1):
                        ref = item(f, k)
                        remote(ref, ref, send.at[f, i, k % 2], recv.at[f, k], to[i]).wait_send()

    def drain_flows():
        @pl.when(c == 0)
        def _():
            drain(top_item, fc_send, fc_recv, TOP_ITEMS)

        drain(long_item, fl_send, fl_recv, KS)

    def drain_copies():
        for copy in core_copies + xin_copies:
            copy.wait_send()

        @pl.when(c == 0)
        def _():
            for copy in trx_copies:
                copy.wait_send()

    q_copy = remote(q, q, q_send, q_recv, other)

    def eliminate():
        for g in range(2):
            acc[g, :, :W] = c1[(4 + 2 * g) * W:(6 + 2 * g) * W].astype(F32)
            acc[g, :W, W:2 * W] = c2[(4 + g) * W:(5 + g) * W].astype(F32)
            acc[g, :W, 2 * W:] = trx[2 * g, W:2 * W].astype(F32) + trx[2 * g + 1, W:2 * W].astype(F32)
            acc[g, W:, W:] = jnp.zeros((W, 2 * W), F32)
            for i in (2 * g, 2 * g + 1):
                rows = jnp.concatenate(
                    [c1[i * W:(i + 1) * W], c2[i * W:(i + 1) * W], trx[i, :W]], axis=1
                )
                vx[i] = pivots(c0[i * SEP_END:i * SEP_END + W], rows, [inv[2 * i, 0], inv[2 * i, 1]])
                acc[g] -= dot(c0[i * SEP_END + W:(i + 1) * SEP_END], vx[i])
        last = [c2[6 * W:].astype(F32), sum(trx[i, 2 * W:].astype(F32) for i in range(NX))]
        last = jnp.concatenate(last, axis=1)
        vg = []
        for g in range(2):
            columns = acc[g, :, :W].astype(BF)
            vg.append(pivots(columns[:W], acc[g, :W, W:].astype(BF), [inv[4 * g + 1, 0], inv[4 * g + 1, 1]]))
            last = last + acc[g, W:, W:] - dot(columns[W:], vg[g])
        last = last.astype(BF)
        vh = pivots(last[:, :W], last[:, W:], [inv[3, 0], inv[3, 1]])
        q[6 * W:] = vh
        for g in range(2):
            qb = (vg[g][:, W:].astype(F32) - dot(vg[g][:, :W], vh)).astype(BF)
            q[(4 + g) * W:(5 + g) * W] = qb
            for i in (2 * g, 2 * g + 1):
                qa = vx[i, :, 2 * W:].astype(F32) - dot(vx[i, :, W:2 * W], vh) - dot(vx[i, :, :W], qb)
                q[i * W:(i + 1) * W] = qa.astype(BF)

    def factor_phase():
        inv_load.wait()

        @pl.when(c == 0)
        def _():
            eliminate()
            q_copy.start()
            q_copy.wait_send()

        @pl.when(c == 1)
        def _():
            q_copy.wait_recv()

    def finish(b, carry):
        n = 256
        here = pl.ds(pl.multiple_of(b * n, n), n)
        total = sum(xin[i, here].astype(F32) for i in range(NX))
        for i in range(7):
            if i < 4:
                block = l0[pl.ds(pl.multiple_of(i * ROWS + b * n, n), n), :]
            elif i < 6:
                block = l1[pl.ds(pl.multiple_of((i - 4) * ROWS + b * n, n), n), :]
            else:
                block = l2[here]
            total = total - dot(block, q[i * W:(i + 1) * W])
        kept = (panel > 2) & ((level > 0) | (b * n >= SEP_END))
        out[here, :] = jnp.where(kept, total, 0.0).astype(BF)
        return carry

    core_phase()
    x_phase()
    flows()
    drain_flows()
    drain_copies()
    factor_phase()
    lax.fori_loop(0, ROWS // 256, finish, 0)


def solution(mesh):
    def body(contrib, pattern, pivot_inverse):
        vmem = pl.BlockSpec(memory_space=pltpu.VMEM)
        anywhere = pl.BlockSpec(memory_space=pl.ANY)
        dma = pltpu.SemaphoreType.DMA
        nf = len(FLOWS)
        return pl.pallas_call(
            kernel,
            out_shape=jax.ShapeDtypeStruct((ROWS, W), BF),
            in_specs=[pl.BlockSpec(memory_space=pltpu.SMEM), anywhere, anywhere],
            out_specs=vmem,
            scratch_shapes=[
                pltpu.VMEM((2 * NX * ROWS, W), BF),
                pltpu.VMEM((8, 2, PANEL, PANEL), BF),
                pltpu.VMEM((NX, ROWS, W), BF),
                pltpu.VMEM((NX, ROWS, W), BF),
                pltpu.VMEM((NX, ROWS, W), BF),
                pltpu.VMEM((NX, ROWS, W), BF),
                pltpu.VMEM((NX, SEP_END, W), BF),
                pltpu.VMEM((4 * ROWS, W), BF),
                pltpu.VMEM((2 * ROWS, W), BF),
                pltpu.VMEM((ROWS, W), BF),
                pltpu.VMEM((NX * SEP_END, W), BF),
                pltpu.VMEM((8 * W, W), BF),
                pltpu.VMEM((7 * W, W), BF),
                pltpu.VMEM((7 * W, W), BF),
                pltpu.VMEM((NX, W, 3 * W), BF),
                pltpu.VMEM((2, 2 * W, 3 * W), F32),
                dma((2 * NX + 1,)), dma((NX,)), dma((NX,)), dma((3,)), dma((NX,)), dma((3,)), dma((NX,)),
                dma((nf, 4, 2)), dma((nf, KC)), dma((nf, 4, 2)), dma((nf, KL)),
                dma, dma,
            ],
            compiler_params=pltpu.CompilerParams(
                collective_id=0, has_side_effects=True, vmem_limit_bytes=56 * 1024 * 1024
            ),
        )(pattern[0], contrib[0], pivot_inverse)

    in_specs = (P("level", None, "panel"), P("level", None, None), P())
    return jax.shard_map(body, mesh=mesh, in_specs=in_specs, out_specs=P("level", "panel"), check_vma=False)
```

time: 156 us -> 100 us (0.64)
  the two profiles are of different devices: /device:TPU:33 before, /device:TPU:1 now
where the time goes in v2:
time: 100 us; the launch traced here: 99.7 us
  Pallas kernels  97.9 us (98%)
  local copies, waits for them, and re-layouts  1.87 us (2%)
    pallas_call x1, Pallas kernels, body(): pl.pallas_call(kernel, out_shape=jax.ShapeDtypeStruct((ROWS, W), BF), in_...  97.9 us

profile of v2, /device:TPU:1, one launch (start us, length us, event | category | flops | bytes accessed | tf_op | source)
XLA Modules:
  0.0 99.7 jit_solution(2833180136688324356)
XLA Ops:
  0.0 97.9 %shard_map.37 = bf16[1024,256]{1,0:T(8,128)(2,1)} custom-call(s32[64,64]{1,0:T(8,128)} %bitcast.3, bf16[8192,256]{1,0:T(8,128)(2,1)} %bitcast.2, bf16[8,2,128,128]{3,2,1,0:T(8,128)(2,1)} %inv_in.1), custom_call_target="tpu_custom_call" | custom-call | tf_op jit(solution)/shard_map/pallas_call | solution.py:387
  97.9 1.9 %copy.5 = bf16[1024,256]{1,0:T(8,128)(2,1)} copy(bf16[1024,256]{1,0:T(8,128)(2,1)} %shard_map.37) | data formatting | bytes 1048576

commit v3 on v0

v3 whole, which is shorter than its diff:
```python
import functools

import jax
import jax.numpy as jnp
import numpy as np
from jax import lax
from jax.experimental import pallas as pl
from jax.experimental.pallas import tpu as pltpu
from jax.sharding import PartitionSpec as P

MESH = pl.DeviceIdType.MESH
PANEL = 128
W = 256
SEP_END = 3 * W
NX, NC, NY, NZ = 4, 2, 4, 8
ROWS = 1024
BF, F32 = jnp.bfloat16, jnp.float32
TREES = (
    ((0xFE000082, 0x657D0001, 0x07440000, 0xE1240000), (0x55AA55AA, 0xC6113992, 0x38FEFE7C)),
    ((0x0080100C, 0x0A80000E, 0x3810387F, 0x028B0600), (0x55AA55AA, 0xE776E4CC, 0xF8FDFBF0)),
    ((0x007DCF01, 0x0000FE00, 0x40080700, 0x0440E100), (0x55AA55AA, 0xBB93C692, 0xFE7C387C)),
    ((0x00022070, 0x900200F0, 0x80A3C000, 0x181018FD), (0x55AA55AA, 0xCFDC4E66, 0x3E7FBF1E)),
)
DEPTH = 7
FIRST = tuple([mask & 1 for mask in go].index(1) for go, _ in TREES)
FLOWS = tuple((slab, tree) for slab in range(3) for tree in range(4))
KC = 4
LONG = (
    ((4, 5, 6, 7, 8, 9, 10, 11), (8, 9, 10, 11), (8, 10)),
    ((0, 1, 6, 7, 8, 9, 10, 11), (8, 9, 10, 11), (8, 10)),
)
TOPS = (0, 1, 2, 3)
CROSS = (0, 1, 2, 3)
HOPS = (6, 6)
SLOTS = 22
LAST = max(max(max(slots) for slots in LONG[i]) + (DEPTH - 1) * HOPS[i] // 2 for i in range(NC)) + 1
ELIMINATE = TOPS[-1] + 1 + (DEPTH - 1) * HOPS[0] // 2


def dot(a, b):
    return jnp.dot(a, b, preferred_element_type=F32)


def bit_of(word, at):
    return lax.shift_right_logical(word, at) & 1


def bit(mask, at):
    return bit_of(jnp.int32(np.uint32(mask).astype(np.int32)), at)


def at_slot(slots, core, slot):
    inside = (slot >= 0) & (slot < SLOTS)
    slot = jnp.clip(slot, 0, SLOTS - 1)
    taken = bit_of(jnp.where(core == 0, *[jnp.int32(sum(1 << t for t in own)) for own in slots]), slot) == 1
    words = [
        jnp.where(core == 0, *[jnp.int32(sum(k << 3 * (t % 10) for k, t in enumerate(own) if t // 10 == w)) for own in slots])
        for w in range(3)
    ]
    word = jnp.where(slot < 10, words[0], jnp.where(slot < 20, words[1], words[2]))
    return inside & taken, lax.shift_right_logical(word, 3 * lax.rem(slot, 10)) & 7


def pivots(fronts):
    seps, rows, inverses = zip(*fronts)
    n = range(len(fronts))
    first = [dot(inverses[i][0], rows[i][:PANEL]).astype(BF) for i in n]
    between = [dot(inverses[i][0], seps[i][:PANEL, PANEL:]).astype(BF) for i in n]
    second = [(rows[i][PANEL:].astype(F32) - dot(seps[i][PANEL:, :PANEL], first[i])).astype(BF) for i in n]
    second = [dot(inverses[i][1], second[i]).astype(BF) for i in n]
    first = [(first[i].astype(F32) - dot(between[i], second[i])).astype(BF) for i in n]
    return [jnp.concatenate([first[i], second[i]], 0) for i in n]


def kernel(
    pattern_in, contrib, inv_in, out,
    pattern, raw, inv, sent, own, xin, fin, trx, first_l, first_c, cross_l, cross_c,
    l0, l1, l2, c0, c1, c2, q, vx, vg, acc,
    load, core_send, core_recv, trx_send, trx_recv, xin_send, xin_recv,
    root_send, first_recv, cross_send, cross_recv, flow_send, c_recv, l_recv0, l_recv1, l_recv2, q_send, q_recv,
):
    level, panel = lax.axis_index("level"), lax.axis_index("panel")
    x, c = level // NC, level % NC
    y, z = panel // NZ, panel % NZ
    other = (x * NC + 1 - c, panel)
    apart = (1, 3, 2)
    theres = [lax.rem(x + d, NX) for d in apart]
    to_x = [(there * NC + c, panel) for there in theres]
    to = [
        (level, lax.rem(y + 1, NY) * NZ + z),
        (level, lax.rem(y + NY - 1, NY) * NZ + z),
        (level, y * NZ + lax.rem(z + 1, NZ)),
        (level, y * NZ + lax.rem(z + NZ - 1, NZ)),
    ]
    barrier = pltpu.get_barrier_semaphore()
    partners = [other] + to_x + to
    for partner in partners:
        pl.semaphore_signal(barrier, inc=1, device_id=partner, device_id_type=MESH)

    def remote(src, dst, send, recv, device):
        return pltpu.make_async_remote_copy(
            src_ref=src, dst_ref=dst, send_sem=send, recv_sem=recv, device_id=device, device_id_type=MESH
        )

    def load_block(i):
        rows = pl.ds(pl.multiple_of((NC * (i % NX) + jnp.where(i < NX, 1 - c, c)) * ROWS, ROWS), ROWS)
        return pltpu.make_async_copy(contrib.at[rows], raw.at[rows], load.at[i])

    pattern_load = pltpu.make_async_copy(pattern_in, pattern, load.at[2 * NX + 1])
    pattern_load.start()
    loads = [load_block(i) for i in range(2 * NX)]
    for copy in loads:
        copy.start()
    inv_load = pltpu.make_async_copy(inv_in, inv, load.at[2 * NX])
    inv_load.start()

    lane = lax.broadcasted_iota(jnp.int32, (1, W), 1)

    def mask_block(target, j, parity):
        def step(i, carry):
            row = (j * NC + parity) * (ROWS // PANEL) + i
            left = pattern[row, panel * 2].astype(F32)
            right = pattern[row, panel * 2 + 1].astype(F32)
            factor = jnp.where(lane < PANEL, left, right)
            block = raw[pl.ds(pl.multiple_of(row * PANEL, PANEL), PANEL), :].astype(F32) * factor
            target[j, i // 2, pl.ds(2 * lax.rem(i, 2), 2)] = block.astype(BF).reshape(2, 64, W)
            return carry

        lax.fori_loop(0, ROWS // PANEL, step, 0)

    core_copies = [remote(sent.at[j], fin.at[j], core_send.at[j], core_recv.at[j], other) for j in range(NX)]

    def add_block(j):
        core_copies[j].wait_recv()
        for h in range(4):
            own[j, h] = (own[j, h].astype(F32) + fin[j, h].astype(F32)).astype(BF)

    places = []
    for slab, tree in FLOWS:
        at = y * NZ + lax.rem(z - slab + NZ, NZ)
        go, deep = TREES[tree]
        depth = bit(deep[0], at) + 2 * bit(deep[1], at) + 4 * bit(deep[2], at)
        places.append((depth, [(bit(mask, at) == 1) & (depth > 0) for mask in go]))
    nexts = []
    for slab in range(3):
        firsts = [places[slab * 4 + tree][0] == 1 for tree in range(4)]
        nexts.append((sum(f.astype(jnp.int32) for f in firsts) > 0, sum(t * f.astype(jnp.int32) for t, f in enumerate(firsts))))
    root = jnp.minimum(panel, 2)

    top_rows = own.at[0, pl.ds(0, 3)]
    trx_copies = [remote(top_rows, trx.at[x], trx_send.at[i], trx_recv.at[x], to_x[i]) for i in range(3)]
    xin_copies = [
        remote(own.at[theres[i]], xin.at[x], xin_send.at[i], xin_recv.at[x], to_x[i]) for i in range(3)
    ]
    root_c = [
        remote(own.at[0, pl.ds(0, 3), t], first_c.at[root], root_send.at[t, NX], first_recv.at[root, NX], to[FIRST[t]])
        for t in range(4)
    ]
    root_l = [
        [
            remote(own.at[j, :, t], first_l.at[root, j], root_send.at[t, i], first_recv.at[root, j], to[FIRST[t]])
            for t in range(4)
        ]
        for i, j in enumerate([x] + theres)
    ]

    def core_phase():
        pattern_load.wait()
        for j in range(NX):
            loads[j].wait()
            mask_block(sent, j, 1 - c)
            if j == 0:
                pl.semaphore_wait(barrier, len(partners))
            core_copies[j].start()
        for j in range(NX):
            loads[NX + j].wait()
            mask_block(own, j, c)
        for j in range(NX):
            add_block(j)

        @pl.when(panel < 3)
        def _():
            @pl.when(c == 0)
            def _():
                for copy in root_c:
                    copy.start()

            for copies in root_l:
                for copy in copies:
                    copy.start()

    def cross_copy(slab, i):
        return remote(
            first_l.at[slab, theres[i]], cross_l.at[slab, x],
            cross_send.at[slab, 0, i], cross_recv.at[slab, 0, x], to_x[i],
        )

    def cross_copy_c(slab, i):
        return remote(
            first_c.at[slab], cross_c.at[slab, x], cross_send.at[slab, 1, i], cross_recv.at[slab, 1, x], to_x[i]
        )

    def wait_first(slab, j):
        remote(own.at[0, :, 0], first_l.at[slab, j], root_send.at[0, 0], first_recv.at[slab, j], to[0]).wait_recv()

    def wait_cross(slab, there):
        remote(
            first_l.at[slab, 0], cross_l.at[slab, there],
            cross_send.at[slab, 0, 0], cross_recv.at[slab, 0, there], to_x[0],
        ).wait_recv()

    def cross_step(slot):
        for slab in range(3):
            @pl.when(nexts[slab][0] & (c == 0) & (slot == CROSS[0]))
            def _():
                remote(
                    own.at[0, pl.ds(0, 3), 0], first_c.at[slab], root_send.at[0, 0], first_recv.at[slab, NX], to[0]
                ).wait_recv()
                for i in range(3):
                    cross_copy_c(slab, i).start()

            for i in range(3):
                @pl.when(nexts[slab][0] & (slot == CROSS[1 + i]))
                def _():
                    wait_first(slab, theres[i])
                    cross_copy(slab, i).start()

        @pl.when((panel > 2) & (slot == max(CROSS) + 1))
        def _():
            @pl.when(c == 0)
            def _():
                for copy in trx_copies:
                    copy.start()

            for copy in xin_copies:
                copy.start()

    def wait_sums():
        @pl.when(panel > 2)
        def _():
            xin[x] = own[x]
            for there in theres:
                remote(own.at[0], xin.at[there], xin_send.at[0], xin_recv.at[there], to_x[0]).wait_recv()

    def plus(*blocks):
        return sum(block.astype(F32) for block in blocks).astype(BF)

    def top_blocks(slab):
        tree = nexts[slab][1]
        cross_c[slab, x] = first_c[slab]
        for there in theres:
            remote(
                first_c.at[slab], cross_c.at[slab, there],
                cross_send.at[slab, 1, 0], cross_recv.at[slab, 1, there], to_x[0],
            ).wait_recv()
        if slab == 0:
            for i in range(NX):
                c0[i, :, tree] = cross_c[0, i]
            return
        ref = (c0, c1, c2)[slab]
        for i in range(NX):
            ref[i, tree] = cross_c[slab, i, 0]
        for g in range(2):
            if slab == 1:
                for h in range(2):
                    c1[4 + 2 * g + h, tree] = plus(cross_c[1, 2 * g, 1 + h], cross_c[1, 2 * g + 1, 1 + h])
            else:
                c2[4 + g, tree] = plus(cross_c[2, 2 * g, 1], cross_c[2, 2 * g + 1, 1])
        if slab == 2:
            c2[6, tree] = plus(*[cross_c[2, i, 2] for i in range(NX)])
            c2[7, tree] = jnp.zeros((64, W), BF)

    def long_sums(slab):
        tree = nexts[slab][1]
        wait_first(slab, x)
        cross_l[slab, x] = first_l[slab, x]
        for there in theres:
            wait_cross(slab, there)
        if slab == 1:
            for g in range(2):
                l1[g, :, tree] = plus(cross_l[1, 2 * g], cross_l[1, 2 * g + 1])
        else:
            l2[:, tree] = plus(*[cross_l[2, i] for i in range(NX)])

    def which(j):
        return lax.rem(x + jnp.where(j == 0, 0, jnp.where(j == 1, 3, j - 1)), NX)

    def prepare(slot):
        cross_step(slot)
        for slab in range(3):
            @pl.when((c == 0) & nexts[slab][0] & (slot == TOPS[0]))
            def _():
                top_blocks(slab)

        for j in range(NX):
            @pl.when(nexts[0][0] & (slot == jnp.where(c == 0, *[LONG[core][0][2 * j] for core in range(NC)])))
            def _():
                there = which(j)
                if j == 0:
                    wait_first(0, x)
                    l0[x, :, nexts[0][1]] = first_l[0, x]
                else:
                    wait_cross(0, there)
                    l0[there, :, nexts[0][1]] = cross_l[0, there]

        for slab in (1, 2):
            @pl.when(nexts[slab][0] & (slot == jnp.where(c == 0, *[LONG[core][slab][0] for core in range(NC)])))
            def _():
                long_sums(slab)

    def top_item(f, k):
        slab, tree = FLOWS[f]
        if slab == 0:
            return c0.at[k, :, tree]
        return (c0, c1, c2)[slab].at[pl.ds(2 * k, 2), tree]

    def long_item(f, k):
        slab, tree = FLOWS[f]
        here = pl.ds(2 * lax.rem(k, 2), 2)
        if slab == 0:
            return l0.at[which(k // 2), here, tree]
        if slab == 1:
            return l1.at[k // 2, here, tree]
        return l2.at[here, tree]

    def handle(f, k, item, recv, row):
        depth, go = places[f]
        ref = item(f, k)

        @pl.when(depth > 1)
        def _():
            remote(ref, ref, flow_send.at[f, 0], recv.at[row, k], to[0]).wait_recv()

        for i in range(4):
            @pl.when(go[i])
            def _():
                remote(ref, ref, flow_send.at[f, i], recv.at[row, k], to[i]).start()

    pieces = []
    hop = jnp.where(c == 0, *HOPS)

    def step(tau, carry):
        prepare(tau)
        for f, (slab, tree) in enumerate(FLOWS):
            depth = places[f][0]
            slot = tau - (depth - 1) * hop // 2
            is_top, k_top = at_slot((TOPS, TOPS), c, slot)
            is_long, k_long = at_slot((LONG[0][slab], LONG[1][slab]), c, slot)

            @pl.when((c == 0) & (depth > 0) & is_top)
            def _():
                handle(f, k_top, top_item, c_recv, f)

            @pl.when((depth > 0) & is_long)
            def _():
                handle(f, k_long, long_item, (l_recv0, l_recv1, l_recv2)[slab], tree)

        for i, piece in enumerate(pieces):
            when = min(ELIMINATE + i * (LAST - ELIMINATE) // len(pieces), LAST - 1)
            pl.when((c == 0) & (panel > 2) & (tau == when))(piece)
        return carry

    def flows():
        lax.fori_loop(0, LAST, step, 0)

    def drain_flows():
        for f, (slab, _) in enumerate(FLOWS):
            long_rows = (4, 2, 1)[slab] * ROWS // 4
            top = (SEP_END, 2 * W, 2 * W)[slab]
            for core, rows in ((0, long_rows + top), (1, long_rows)):
                for i in range(4):
                    @pl.when(places[f][1][i] & (c == core))
                    def _():
                        sized = raw.at[pl.ds(0, rows)]
                        remote(sized, sized, flow_send.at[f, i], c_recv.at[f, 0], to[i]).wait_send()

    q_copy = remote(q, q, q_send, q_recv, other)

    def drain_copies():
        for copy in core_copies:
            copy.wait_send()

        @pl.when(panel < 3)
        def _():
            for copies in root_l:
                for copy in copies:
                    copy.wait_send()

            @pl.when(c == 0)
            def _():
                for copy in root_c:
                    copy.wait_send()

        for slab in range(3):
            @pl.when(nexts[slab][0])
            def _():
                for i in range(3):
                    cross_copy(slab, i).wait_send()

                @pl.when(c == 0)
                def _():
                    for i in range(3):
                        cross_copy_c(slab, i).wait_send()

        @pl.when(panel > 2)
        def _():
            for copy in xin_copies:
                copy.wait_send()

            @pl.when(c == 0)
            def _():
                q_copy.wait_send()
                for copy in trx_copies:
                    copy.wait_send()

    def flat(block):
        return block.reshape(-1, W)

    def wait_top():
        inv_load.wait()
        trx[x] = own[0, :3]
        for there in theres:
            remote(top_rows, trx.at[there], trx_send.at[0], trx_recv.at[there], to_x[0]).wait_recv()

    def front_weights(g):
        pair = (2 * g, 2 * g + 1)
        fronts = []
        for i in pair:
            rows = jnp.concatenate([flat(c1[i]), flat(c2[i]), flat(trx[i, 0])], axis=1)
            fronts.append((flat(c0[i, 0]), rows, [inv[2 * i, 0], inv[2 * i, 1]]))
        for i, weights in zip(pair, pivots(fronts)):
            vx[i] = weights

    def front_update(i):
        g = i // 2
        if i % 2 == 0:
            acc[g, :, :W] = flat(c1[4 + 2 * g:6 + 2 * g]).astype(F32)
            acc[g, :W, W:2 * W] = flat(c2[4 + g]).astype(F32)
            acc[g, :W, 2 * W:] = flat(trx[2 * g, 1]).astype(F32) + flat(trx[2 * g + 1, 1]).astype(F32)
            acc[g, W:, W:] = jnp.zeros((W, 2 * W), F32)
        acc[g] -= dot(flat(c0[i, 1:]), vx[i])

    def pair_weights():
        columns = [acc[g, :, :W].astype(BF) for g in range(2)]
        fronts = [
            (columns[g][:W], acc[g, :W, W:].astype(BF), [inv[4 * g + 1, 0], inv[4 * g + 1, 1]]) for g in range(2)
        ]
        for g, weights in enumerate(pivots(fronts)):
            vg[g] = weights
            acc[g, W:, W:] -= dot(columns[g][W:], weights)

    def last_weights():
        last = [flat(c2[6]).astype(F32), sum(flat(trx[i, 2]).astype(F32) for i in range(NX))]
        last = (jnp.concatenate(last, axis=1) + acc[0, W:, W:] + acc[1, W:, W:]).astype(BF)
        q[6 * W:] = pivots([(last[:, :W], last[:, W:], [inv[3, 0], inv[3, 1]])])[0]

    def pair_factor():
        vh = q[6 * W:]
        for g in range(2):
            q[(4 + g) * W:(5 + g) * W] = (vg[g, :, W:].astype(F32) - dot(vg[g, :, :W], vh)).astype(BF)

    def front_factor(g):
        vh, qb = q[6 * W:], q[(4 + g) * W:(5 + g) * W]
        for i in (2 * g, 2 * g + 1):
            total = vx[i, :, 2 * W:].astype(F32) - dot(vx[i, :, W:2 * W], vh)
            q[i * W:(i + 1) * W] = (total - dot(vx[i, :, :W], qb)).astype(BF)

    pieces.append(wait_top)
    for g in range(2):
        pieces.append(functools.partial(front_weights, g))
        pieces += [functools.partial(front_update, 2 * g + i) for i in range(2)]
    pieces += [pair_weights, last_weights, pair_factor]
    pieces += [functools.partial(front_factor, g) for g in range(2)] + [q_copy.start]

    def finish(b, carry):
        n = 256
        total = sum(flat(xin[i, b]).astype(F32) for i in range(NX))
        for i in range(7):
            block = l0[i, b] if i < 4 else l1[i - 4, b] if i < 6 else l2[b]
            total = total - dot(flat(block), q[i * W:(i + 1) * W])
        kept = (level > 0) | (b * n >= SEP_END)
        out[pl.ds(pl.multiple_of(b * n, n), n), :] = jnp.where(kept, total, 0.0).astype(BF)
        return carry

    def result():
        @pl.when(panel < 3)
        def _():
            inv_load.wait()
            out[...] = jnp.zeros_like(out)

        @pl.when(panel > 2)
        def _():
            @pl.when(c == 1)
            def _():
                inv_load.wait()
                q_copy.wait_recv()

            lax.fori_loop(0, ROWS // 256, finish, 0)

    core_phase()
    flows()
    wait_sums()
    result()
    drain_flows()
    drain_copies()


def solution(mesh):
    def body(contrib, pattern, pivot_inverse):
        anywhere = pl.BlockSpec(memory_space=pl.ANY)
        dma = pltpu.SemaphoreType.DMA
        nf = len(FLOWS)

        def rows(*sizes):
            return pltpu.VMEM((*sizes, 64, W), BF)

        return pl.pallas_call(
            kernel,
            out_shape=jax.ShapeDtypeStruct((ROWS, W), BF),
            in_specs=[anywhere] * 3,
            out_specs=pl.BlockSpec(memory_space=pltpu.VMEM),
            scratch_shapes=[
                pltpu.SMEM((64, 64), jnp.int32),
                pltpu.VMEM((2 * NX * ROWS, W), BF),
                pltpu.VMEM((8, 2, PANEL, PANEL), BF),
                rows(NX, 4, 4), rows(NX, 4, 4), rows(NX, 4, 4), rows(NX, 4, 4), rows(NX, 3, 4),
                rows(3, NX, 4), rows(3, 3), rows(3, NX, 4), rows(3, NX, 3),
                rows(4, 4, 4), rows(2, 4, 4), rows(4, 4), rows(NX, 3, 4), rows(8, 4), rows(8, 4),
                pltpu.VMEM((7 * W, W), BF),
                pltpu.VMEM((NX, W, 3 * W), BF),
                pltpu.VMEM((2, W, 2 * W), BF),
                pltpu.VMEM((2, 2 * W, 3 * W), F32),
                dma((2 * NX + 2,)), dma((NX,)), dma((NX,)), dma((3,)), dma((NX,)), dma((3,)), dma((NX,)),
                dma((4, NX + 1)), dma((3, NX + 1)), dma((3, 2, 3)), dma((3, 2, NX)),
                dma((nf, 4)), dma((nf, KC)), dma((4, 8)), dma((4, 4)), dma((4, 2)),
                dma, dma,
            ],
            compiler_params=pltpu.CompilerParams(
                collective_id=0, has_side_effects=True, vmem_limit_bytes=56 * 1024 * 1024
            ),
        )(pattern[0], contrib[0], pivot_inverse)

    in_specs = (P("level", None, "panel"), P("level", None, None), P())
    return jax.shard_map(body, mesh=mesh, in_specs=in_specs, out_specs=P("level", "panel"), check_vma=False)
```

time: 1230 us -> 87.7 us (0.07)
  the two profiles are of different devices: /device:TPU:2 before, /device:TPU:9 now
where the time goes in v3:
time: 87.7 us; the launch traced here: 87.6 us
  Pallas kernels  85.7 us (98%)
  local copies, waits for them, and re-layouts  1.87 us (2%)
    pallas_call x1, Pallas kernels, body(): pl.pallas_call(kernel, out_shape=jax.ShapeDtypeStruct((ROWS, W), BF), in_...  85.7 us
    unnamed x1, local copies, waits for them, and re-layouts  1.87 us

profile of v3, /device:TPU:9, one launch (start us, length us, event | category | flops | bytes accessed | tf_op | source)
XLA Modules:
  0.0 87.6 jit_solution(9435977907073576785)
XLA Ops:
  0.0 85.7 %shard_map.37 = bf16[1024,256]{1,0:T(8,128)(2,1)} custom-call(s32[64,64]{1,0:T(8,128)} %bitcast.3, bf16[8192,256]{1,0:T(8,128)(2,1)} %bitcast.2, bf16[8,2,128,128]{3,2,1,0:T(8,128)(2,1)} %inv_in.1), custom_call_target="tpu_custom_call" | custom-call | tf_op jit(solution)/shard_map/pallas_call | solution.py:517
  85.7 1.9 %copy.5 = bf16[1024,256]{1,0:T(8,128)(2,1)} copy(bf16[1024,256]{1,0:T(8,128)(2,1)} %shard_map.37) | data formatting | bytes 1048576

commit v4 on v3

--- a/solution.py
+++ b/solution.py
@@ -26,15 +26,17 @@
 FLOWS = tuple((slab, tree) for slab in range(3) for tree in range(4))
 KC = 4
 LONG = (
-    ((4, 5, 6, 7, 8, 9, 10, 11), (8, 9, 10, 11), (8, 10)),
+    ((5, 6, 7, 8, 9, 10, 11, 12), (9, 10, 11, 12), (9, 11)),
     ((0, 1, 6, 7, 8, 9, 10, 11), (8, 9, 10, 11), (8, 10)),
 )
-TOPS = (0, 1, 2, 3)
+TOPS = ((0, 1, 2, 3), (1, 2, 3, 4), (1, 2, 3, 4))
 CROSS = (0, 1, 2, 3)
-HOPS = (6, 6)
+HOPS = (6, 4)
 SLOTS = 22
 LAST = max(max(max(slots) for slots in LONG[i]) + (DEPTH - 1) * HOPS[i] // 2 for i in range(NC)) + 1
-ELIMINATE = TOPS[-1] + 1 + (DEPTH - 1) * HOPS[0] // 2
+ELIMINATE = max(max(slots) for slots in TOPS) + 1 + (DEPTH - 1) * HOPS[0] // 2
+UNROLL = 1
+SPREAD = 3
 
 
 def dot(a, b):
@@ -50,15 +52,13 @@
 
 
 def at_slot(slots, core, slot):
-    inside = (slot >= 0) & (slot < SLOTS)
-    slot = jnp.clip(slot, 0, SLOTS - 1)
     taken = bit_of(jnp.where(core == 0, *[jnp.int32(sum(1 << t for t in own)) for own in slots]), slot) == 1
     words = [
         jnp.where(core == 0, *[jnp.int32(sum(k << 3 * (t % 10) for k, t in enumerate(own) if t // 10 == w)) for own in slots])
         for w in range(3)
     ]
     word = jnp.where(slot < 10, words[0], jnp.where(slot < 20, words[1], words[2]))
-    return inside & taken, lax.shift_right_logical(word, 3 * lax.rem(slot, 10)) & 7
+    return taken, lax.shift_right_logical(word, 3 * lax.rem(slot, 10)) & 7
 
 
 def pivots(fronts):
@@ -102,8 +102,12 @@
             src_ref=src, dst_ref=dst, send_sem=send, recv_sem=recv, device_id=device, device_id_type=MESH
         )
 
+    near = [x] + theres
+    top_at = jnp.where(x == 0, 0, jnp.where(x == 3, 1, jnp.where(x == 1, 2, 3)))
+    order = [0] + [jnp.where(top_at >= n, near[n - 1], near[n]) for n in range(1, NX)]
+
     def load_block(i):
-        rows = pl.ds(pl.multiple_of((NC * (i % NX) + jnp.where(i < NX, 1 - c, c)) * ROWS, ROWS), ROWS)
+        rows = pl.ds(pl.multiple_of((NC * order[i % NX] + jnp.where(i < NX, 1 - c, c)) * ROWS, ROWS), ROWS)
         return pltpu.make_async_copy(contrib.at[rows], raw.at[rows], load.at[i])
 
     pattern_load = pltpu.make_async_copy(pattern_in, pattern, load.at[2 * NX + 1])
@@ -114,26 +118,39 @@
     inv_load = pltpu.make_async_copy(inv_in, inv, load.at[2 * NX])
     inv_load.start()
 
-    lane = lax.broadcasted_iota(jnp.int32, (1, W), 1)
-
-    def mask_block(target, j, parity):
+    lane = lax.broadcasted_iota(jnp.int32, (PANEL, W), 1)
+
+    def mask_block(j, parity, store):
         def step(i, carry):
             row = (j * NC + parity) * (ROWS // PANEL) + i
             left = pattern[row, panel * 2].astype(F32)
             right = pattern[row, panel * 2 + 1].astype(F32)
-            factor = jnp.where(lane < PANEL, left, right)
-            block = raw[pl.ds(pl.multiple_of(row * PANEL, PANEL), PANEL), :].astype(F32) * factor
-            target[j, i // 2, pl.ds(2 * lax.rem(i, 2), 2)] = block.astype(BF).reshape(2, 64, W)
+            factor = jnp.where(lane < PANEL, left, right).astype(BF)
+            block = raw[pl.ds(pl.multiple_of(row * PANEL, PANEL), PANEL), :] * factor
+            store(i // 2, pl.ds(2 * lax.rem(i, 2), 2), block.reshape(2, 64, W))
             return carry
 
-        lax.fori_loop(0, ROWS // PANEL, step, 0)
-
-    core_copies = [remote(sent.at[j], fin.at[j], core_send.at[j], core_recv.at[j], other) for j in range(NX)]
-
-    def add_block(j):
-        core_copies[j].wait_recv()
-        for h in range(4):
-            own[j, h] = (own[j, h].astype(F32) + fin[j, h].astype(F32)).astype(BF)
+        lax.fori_loop(0, ROWS // PANEL, step, 0, unroll=UNROLL)
+
+    core_copies = [remote(sent.at[j], fin.at[j], core_send.at[n], core_recv.at[n], other) for n, j in enumerate(order)]
+
+    def send_block(n):
+        def store(h, half, block):
+            sent[order[n], h, half] = block
+
+        loads[n].wait()
+        mask_block(order[n], 1 - c, store)
+        if n == 0:
+            pl.semaphore_wait(barrier, len(partners))
+        core_copies[n].start()
+
+    def add_block(n):
+        def store(h, half, block):
+            own[order[n], h, half] = block + fin[order[n], h, half]
+
+        loads[NX + n].wait()
+        core_copies[n].wait_recv()
+        mask_block(order[n], c, store)
 
     places = []
     for slab, tree in FLOWS:
@@ -158,35 +175,28 @@
     ]
     root_l = [
         [
-            remote(own.at[j, :, t], first_l.at[root, j], root_send.at[t, i], first_recv.at[root, j], to[FIRST[t]])
+            remote(own.at[j, :, t], first_l.at[root, j], root_send.at[t, n], first_recv.at[root, j], to[FIRST[t]])
             for t in range(4)
         ]
-        for i, j in enumerate([x] + theres)
+        for n, j in enumerate(order)
     ]
 
     def core_phase():
         pattern_load.wait()
-        for j in range(NX):
-            loads[j].wait()
-            mask_block(sent, j, 1 - c)
-            if j == 0:
-                pl.semaphore_wait(barrier, len(partners))
-            core_copies[j].start()
-        for j in range(NX):
-            loads[NX + j].wait()
-            mask_block(own, j, c)
-        for j in range(NX):
-            add_block(j)
-
-        @pl.when(panel < 3)
-        def _():
-            @pl.when(c == 0)
-            def _():
-                for copy in root_c:
-                    copy.start()
-
-            for copies in root_l:
-                for copy in copies:
+        for n in range(NX):
+            send_block(n)
+        for n in range(NX):
+            add_block(n)
+
+            @pl.when(panel < 3)
+            def _():
+                if n == 0:
+                    @pl.when(c == 0)
+                    def _():
+                        for copy in root_c:
+                            copy.start()
+
+                for copy in root_l[n]:
                     copy.start()
 
     def cross_copy(slab, i):
@@ -225,15 +235,14 @@
                     wait_first(slab, theres[i])
                     cross_copy(slab, i).start()
 
-        @pl.when((panel > 2) & (slot == max(CROSS) + 1))
-        def _():
-            @pl.when(c == 0)
-            def _():
-                for copy in trx_copies:
-                    copy.start()
-
-            for copy in xin_copies:
+    def x_start():
+        @pl.when(c == 0)
+        def _():
+            for copy in trx_copies:
                 copy.start()
+
+        for copy in xin_copies:
+            copy.start()
 
     def wait_sums():
         @pl.when(panel > 2)
@@ -244,19 +253,18 @@
 
     def plus(*blocks):
         return sum(block.astype(F32) for block in blocks).astype(BF)
+
+    def wait_cross_c(slab, there):
+        remote(
+            first_c.at[slab], cross_c.at[slab, there],
+            cross_send.at[slab, 1, 0], cross_recv.at[slab, 1, there], to_x[0],
+        ).wait_recv()
 
     def top_blocks(slab):
         tree = nexts[slab][1]
         cross_c[slab, x] = first_c[slab]
         for there in theres:
-            remote(
-                first_c.at[slab], cross_c.at[slab, there],
-                cross_send.at[slab, 1, 0], cross_recv.at[slab, 1, there], to_x[0],
-            ).wait_recv()
-        if slab == 0:
-            for i in range(NX):
-                c0[i, :, tree] = cross_c[0, i]
-            return
+            wait_cross_c(slab, there)
         ref = (c0, c1, c2)[slab]
         for i in range(NX):
             ref[i, tree] = cross_c[slab, i, 0]
@@ -287,8 +295,18 @@
 
     def prepare(slot):
         cross_step(slot)
-        for slab in range(3):
-            @pl.when((c == 0) & nexts[slab][0] & (slot == TOPS[0]))
+        for j in range(NX):
+            @pl.when((c == 0) & nexts[0][0] & (slot == TOPS[0][j]))
+            def _():
+                there = which(j)
+                if j == 0:
+                    c0[x, :, nexts[0][1]] = first_c[0]
+                else:
+                    wait_cross_c(0, there)
+                    c0[there, :, nexts[0][1]] = cross_c[0, there]
+
+        for slab in (1, 2):
+            @pl.when((c == 0) & nexts[slab][0] & (slot == TOPS[slab][0]))
             def _():
                 top_blocks(slab)
 
@@ -311,7 +329,7 @@
     def top_item(f, k):
         slab, tree = FLOWS[f]
         if slab == 0:
-            return c0.at[k, :, tree]
+            return c0.at[which(k), :, tree]
         return (c0, c1, c2)[slab].at[pl.ds(2 * k, 2), tree]
 
     def long_item(f, k):
@@ -337,27 +355,35 @@
                 remote(ref, ref, flow_send.at[f, i], recv.at[row, k], to[i]).start()
 
     pieces = []
+    is_first = nexts[0][0] | nexts[1][0] | nexts[2][0]
     hop = jnp.where(c == 0, *HOPS)
 
     def step(tau, carry):
-        prepare(tau)
+        pl.when(is_first & (tau < SLOTS))(functools.partial(prepare, tau))
+        pl.when((panel > 2) & (tau == max(CROSS) + 1))(x_start)
         for f, (slab, tree) in enumerate(FLOWS):
             depth = places[f][0]
             slot = tau - (depth - 1) * hop // 2
-            is_top, k_top = at_slot((TOPS, TOPS), c, slot)
-            is_long, k_long = at_slot((LONG[0][slab], LONG[1][slab]), c, slot)
-
-            @pl.when((c == 0) & (depth > 0) & is_top)
-            def _():
-                handle(f, k_top, top_item, c_recv, f)
-
-            @pl.when((depth > 0) & is_long)
-            def _():
-                handle(f, k_long, long_item, (l_recv0, l_recv1, l_recv2)[slab], tree)
-
-        for i, piece in enumerate(pieces):
-            when = min(ELIMINATE + i * (LAST - ELIMINATE) // len(pieces), LAST - 1)
-            pl.when((c == 0) & (panel > 2) & (tau == when))(piece)
+
+            @pl.when((depth > 0) & (slot >= 0) & (slot < SLOTS))
+            def _():
+                is_top, k_top = at_slot((TOPS[slab],) * NC, c, slot)
+                is_long, k_long = at_slot((LONG[0][slab], LONG[1][slab]), c, slot)
+
+                @pl.when((c == 0) & is_top)
+                def _():
+                    handle(f, k_top, top_item, c_recv, f)
+
+                @pl.when(is_long)
+                def _():
+                    handle(f, k_long, long_item, (l_recv0, l_recv1, l_recv2)[slab], tree)
+
+        @pl.when((c == 0) & (panel > 2) & (tau >= ELIMINATE))
+        def _():
+            for i, piece in enumerate(pieces):
+                when = min(ELIMINATE + i * SPREAD // len(pieces), LAST - 1)
+                pl.when(tau == when)(piece)
+
         return carry
 
     def flows():

time: 87.7 us -> 79.4 us (0.905)
  the two profiles are of different devices: /device:TPU:9 before, /device:TPU:2 now
where the time goes in v4:
time: 79.4 us; the launch traced here: 78.7 us
  Pallas kernels  76.8 us (97%)
  local copies, waits for them, and re-layouts  1.87 us (2%)
    pallas_call x1, Pallas kernels, body(): pl.pallas_call(kernel, out_shape=jax.ShapeDtypeStruct((ROWS, W), BF), in_...  76.8 us
    unnamed x1, local copies, waits for them, and re-layouts  1.87 us

profile of v4, /device:TPU:2, one launch (start us, length us, event | category | flops | bytes accessed | tf_op | source)
XLA Modules:
  0.0 78.7 jit_solution(14583364651946622894)
XLA Ops:
  0.0 76.8 %shard_map.37 = bf16[1024,256]{1,0:T(8,128)(2,1)} custom-call(s32[64,64]{1,0:T(8,128)} %bitcast.3, bf16[8192,256]{1,0:T(8,128)(2,1)} %bitcast.2, bf16[8,2,128,128]{3,2,1,0:T(8,128)(2,1)} %inv_in.1), custom_call_target="tpu_custom_call" | custom-call | tf_op jit(solution)/shard_map/pallas_call | solution.py:543
  76.8 1.9 %copy.5 = bf16[1024,256]{1,0:T(8,128)(2,1)} copy(bf16[1024,256]{1,0:T(8,128)(2,1)} %shard_map.37) | data formatting | bytes 1048576

commit v5 on v4

--- a/solution.py
+++ b/solution.py
@@ -26,8 +26,8 @@
 FLOWS = tuple((slab, tree) for slab in range(3) for tree in range(4))
 KC = 4
 LONG = (
-    ((5, 6, 7, 8, 9, 10, 11, 12), (9, 10, 11, 12), (9, 11)),
-    ((0, 1, 6, 7, 8, 9, 10, 11), (8, 9, 10, 11), (8, 10)),
+    ((5, 6, 7, 9, 10, 11, 12, 13), (9, 10, 11, 12), (9, 11)),
+    ((0, 1, 4, 5, 7, 8, 10, 11), (6, 7, 9, 10), (8, 11)),
 )
 TOPS = ((0, 1, 2, 3), (1, 2, 3, 4), (1, 2, 3, 4))
 CROSS = (0, 1, 2, 3)
@@ -83,7 +83,7 @@
     x, c = level // NC, level % NC
     y, z = panel // NZ, panel % NZ
     other = (x * NC + 1 - c, panel)
-    apart = (1, 3, 2)
+    apart = (2, 1, 3)
     theres = [lax.rem(x + d, NX) for d in apart]
     to_x = [(there * NC + c, panel) for there in theres]
     to = [
@@ -94,8 +94,6 @@
     ]
     barrier = pltpu.get_barrier_semaphore()
     partners = [other] + to_x + to
-    for partner in partners:
-        pl.semaphore_signal(barrier, inc=1, device_id=partner, device_id_type=MESH)
 
     def remote(src, dst, send, recv, device):
         return pltpu.make_async_remote_copy(
@@ -103,7 +101,7 @@
         )
 
     near = [x] + theres
-    top_at = jnp.where(x == 0, 0, jnp.where(x == 3, 1, jnp.where(x == 1, 2, 3)))
+    top_at = jnp.where(x == 0, 0, jnp.where(x == 2, 1, jnp.where(x == 3, 2, 3)))
     order = [0] + [jnp.where(top_at >= n, near[n - 1], near[n]) for n in range(1, NX)]
 
     def load_block(i):
@@ -117,6 +115,8 @@
         copy.start()
     inv_load = pltpu.make_async_copy(inv_in, inv, load.at[2 * NX])
     inv_load.start()
+    for partner in partners:
+        pl.semaphore_signal(barrier, inc=1, device_id=partner, device_id_type=MESH)
 
     lane = lax.broadcasted_iota(jnp.int32, (PANEL, W), 1)
 
@@ -165,17 +165,17 @@
     root = jnp.minimum(panel, 2)
 
     top_rows = own.at[0, pl.ds(0, 3)]
-    trx_copies = [remote(top_rows, trx.at[x], trx_send.at[i], trx_recv.at[x], to_x[i]) for i in range(3)]
+    trx_copies = [remote(top_rows, trx.at[x], trx_send, trx_recv.at[x], to_x[i]) for i in range(3)]
     xin_copies = [
-        remote(own.at[theres[i]], xin.at[x], xin_send.at[i], xin_recv.at[x], to_x[i]) for i in range(3)
+        remote(own.at[theres[i]], xin.at[x], xin_send, xin_recv.at[x], to_x[i]) for i in range(3)
     ]
     root_c = [
-        remote(own.at[0, pl.ds(0, 3), t], first_c.at[root], root_send.at[t, NX], first_recv.at[root, NX], to[FIRST[t]])
+        remote(own.at[0, pl.ds(0, 3), t], first_c.at[root], root_send.at[t], first_recv.at[root, NX], to[FIRST[t]])
         for t in range(4)
     ]
     root_l = [
         [
-            remote(own.at[j, :, t], first_l.at[root, j], root_send.at[t, n], first_recv.at[root, j], to[FIRST[t]])
+            remote(own.at[j, :, t], first_l.at[root, j], root_send.at[t], first_recv.at[root, j], to[FIRST[t]])
             for t in range(4)
         ]
         for n, j in enumerate(order)
@@ -202,21 +202,21 @@
     def cross_copy(slab, i):
         return remote(
             first_l.at[slab, theres[i]], cross_l.at[slab, x],
-            cross_send.at[slab, 0, i], cross_recv.at[slab, 0, x], to_x[i],
+            cross_send.at[slab], cross_recv.at[slab, 0, x], to_x[i],
         )
 
     def cross_copy_c(slab, i):
         return remote(
-            first_c.at[slab], cross_c.at[slab, x], cross_send.at[slab, 1, i], cross_recv.at[slab, 1, x], to_x[i]
+            first_c.at[slab], cross_c.at[slab, x], cross_send.at[slab], cross_recv.at[slab, 1, x], to_x[i]
         )
 
     def wait_first(slab, j):
-        remote(own.at[0, :, 0], first_l.at[slab, j], root_send.at[0, 0], first_recv.at[slab, j], to[0]).wait_recv()
+        remote(own.at[0, :, 0], first_l.at[slab, j], root_send.at[0], first_recv.at[slab, j], to[0]).wait_recv()
 
     def wait_cross(slab, there):
         remote(
             first_l.at[slab, 0], cross_l.at[slab, there],
-            cross_send.at[slab, 0, 0], cross_recv.at[slab, 0, there], to_x[0],
+            cross_send.at[slab], cross_recv.at[slab, 0, there], to_x[0],
         ).wait_recv()
 
     def cross_step(slot):
@@ -224,7 +224,7 @@
             @pl.when(nexts[slab][0] & (c == 0) & (slot == CROSS[0]))
             def _():
                 remote(
-                    own.at[0, pl.ds(0, 3), 0], first_c.at[slab], root_send.at[0, 0], first_recv.at[slab, NX], to[0]
+                    own.at[0, pl.ds(0, 3), 0], first_c.at[slab], root_send.at[0], first_recv.at[slab, NX], to[0]
                 ).wait_recv()
                 for i in range(3):
                     cross_copy_c(slab, i).start()
@@ -249,7 +249,7 @@
         def _():
             xin[x] = own[x]
             for there in theres:
-                remote(own.at[0], xin.at[there], xin_send.at[0], xin_recv.at[there], to_x[0]).wait_recv()
+                remote(own.at[0], xin.at[there], xin_send, xin_recv.at[there], to_x[0]).wait_recv()
 
     def plus(*blocks):
         return sum(block.astype(F32) for block in blocks).astype(BF)
@@ -257,7 +257,7 @@
     def wait_cross_c(slab, there):
         remote(
             first_c.at[slab], cross_c.at[slab, there],
-            cross_send.at[slab, 1, 0], cross_recv.at[slab, 1, there], to_x[0],
+            cross_send.at[slab], cross_recv.at[slab, 1, there], to_x[0],
         ).wait_recv()
 
     def top_blocks(slab):
@@ -291,7 +291,7 @@
             l2[:, tree] = plus(*[cross_l[2, i] for i in range(NX)])
 
     def which(j):
-        return lax.rem(x + jnp.where(j == 0, 0, jnp.where(j == 1, 3, j - 1)), NX)
+        return lax.rem(x + jnp.where(j == 0, 0, jnp.where(j == 1, 2, jnp.where(j == 2, 3, 1))), NX)
 
     def prepare(slot):
         cross_step(slot)
@@ -403,41 +403,35 @@
     q_copy = remote(q, q, q_send, q_recv, other)
 
     def drain_copies():
+        def drain(send, rows):
+            for core in range(NC):
+                @pl.when(c == core)
+                def _():
+                    sized = raw.at[pl.ds(0, rows[core])]
+                    remote(sized, sized, send, q_recv, other).wait_send()
+
         for copy in core_copies:
             copy.wait_send()
 
         @pl.when(panel < 3)
         def _():
-            for copies in root_l:
-                for copy in copies:
-                    copy.wait_send()
-
-            @pl.when(c == 0)
-            def _():
-                for copy in root_c:
-                    copy.wait_send()
+            for t in range(4):
+                drain(root_send.at[t], (ROWS + SEP_END // 4, ROWS))
 
         for slab in range(3):
             @pl.when(nexts[slab][0])
             def _():
-                for i in range(3):
-                    cross_copy(slab, i).wait_send()
-
-                @pl.when(c == 0)
-                def _():
-                    for i in range(3):
-                        cross_copy_c(slab, i).wait_send()
+                drain(cross_send.at[slab], (3 * (ROWS + SEP_END) // 4, 3 * ROWS // 4))
 
         @pl.when(panel > 2)
         def _():
-            for copy in xin_copies:
-                copy.wait_send()
+            drain(xin_send, (3 * ROWS, 3 * ROWS))
 
             @pl.when(c == 0)
             def _():
                 q_copy.wait_send()
-                for copy in trx_copies:
-                    copy.wait_send()
+                sized = raw.at[pl.ds(0, 3 * SEP_END)]
+                remote(sized, sized, trx_send, q_recv, other).wait_send()
 
     def flat(block):
         return block.reshape(-1, W)
@@ -446,7 +440,7 @@
         inv_load.wait()
         trx[x] = own[0, :3]
         for there in theres:
-            remote(top_rows, trx.at[there], trx_send.at[0], trx_recv.at[there], to_x[0]).wait_recv()
+            remote(top_rows, trx.at[there], trx_send, trx_recv.at[there], to_x[0]).wait_recv()
 
     def front_weights(g):
         pair = (2 * g, 2 * g + 1)
@@ -556,8 +550,8 @@
                 pltpu.VMEM((NX, W, 3 * W), BF),
                 pltpu.VMEM((2, W, 2 * W), BF),
                 pltpu.VMEM((2, 2 * W, 3 * W), F32),
-                dma((2 * NX + 2,)), dma((NX,)), dma((NX,)), dma((3,)), dma((NX,)), dma((3,)), dma((NX,)),
-                dma((4, NX + 1)), dma((3, NX + 1)), dma((3, 2, 3)), dma((3, 2, NX)),
+                dma((2 * NX + 2,)), dma((NX,)), dma((NX,)), dma, dma((NX,)), dma, dma((NX,)),
+                dma((4,)), dma((3, NX + 1)), dma((3,)), dma((3, 2, NX)),
                 dma((nf, 4)), dma((nf, KC)), dma((4, 8)), dma((4, 4)), dma((4, 2)),
                 dma, dma,
             ],

time: 79.4 us -> 78.7 us (level)
  no operation moved by 1% of the time
where the time goes in v5:
time: 78.7 us; the launch traced here: 78 us
  Pallas kernels  76.1 us (97%)
  local copies, waits for them, and re-layouts  1.87 us (2%)
    pallas_call x1, Pallas kernels, body(): pl.pallas_call(kernel, out_shape=jax.ShapeDtypeStruct((ROWS, W), BF), in_...  76.1 us
    unnamed x1, local copies, waits for them, and re-layouts  1.87 us

profile of v5, /device:TPU:2, one launch (start us, length us, event | category | flops | bytes accessed | tf_op | source)
XLA Modules:
  0.0 78.0 jit_solution(2418505616465435092)
XLA Ops:
  0.0 76.1 %shard_map.37 = bf16[1024,256]{1,0:T(8,128)(2,1)} custom-call(s32[64,64]{1,0:T(8,128)} %bitcast.3, bf16[8192,256]{1,0:T(8,128)(2,1)} %bitcast.2, bf16[8,2,128,128]{3,2,1,0:T(8,128)(2,1)} %inv_in.1), custom_call_target="tpu_custom_call" | custom-call | tf_op jit(solution)/shard_map/pallas_call | solution.py:537
  76.1 1.9 %copy.5 = bf16[1024,256]{1,0:T(8,128)(2,1)} copy(bf16[1024,256]{1,0:T(8,128)(2,1)} %shard_map.37) | data formatting | bytes 1048576

commit v6 on v5

--- a/solution.py
+++ b/solution.py
@@ -132,7 +132,7 @@
 
         lax.fori_loop(0, ROWS // PANEL, step, 0, unroll=UNROLL)
 
-    core_copies = [remote(sent.at[j], fin.at[j], core_send.at[n], core_recv.at[n], other) for n, j in enumerate(order)]
+    core_copies = [remote(sent.at[j], fin.at[j], core_send, core_recv.at[n], other) for n, j in enumerate(order)]
 
     def send_block(n):
         def store(h, half, block):
@@ -281,14 +281,15 @@
     def long_sums(slab):
         tree = nexts[slab][1]
         wait_first(slab, x)
-        cross_l[slab, x] = first_l[slab, x]
+        if slab == 1:
+            cross_l[slab, x] = first_l[slab, x]
         for there in theres:
             wait_cross(slab, there)
         if slab == 1:
             for g in range(2):
                 l1[g, :, tree] = plus(cross_l[1, 2 * g], cross_l[1, 2 * g + 1])
         else:
-            l2[:, tree] = plus(*[cross_l[2, i] for i in range(NX)])
+            l2[:, tree] = plus(first_l[2, x], *[cross_l[2, there] for there in theres])
 
     def which(j):
         return lax.rem(x + jnp.where(j == 0, 0, jnp.where(j == 1, 2, jnp.where(j == 2, 3, 1))), NX)
@@ -410,8 +411,7 @@
                     sized = raw.at[pl.ds(0, rows[core])]
                     remote(sized, sized, send, q_recv, other).wait_send()
 
-        for copy in core_copies:
-            copy.wait_send()
+        drain(core_send, (NX * ROWS, NX * ROWS))
 
         @pl.when(panel < 3)
         def _():
@@ -550,7 +550,7 @@
                 pltpu.VMEM((NX, W, 3 * W), BF),
                 pltpu.VMEM((2, W, 2 * W), BF),
                 pltpu.VMEM((2, 2 * W, 3 * W), F32),
-                dma((2 * NX + 2,)), dma((NX,)), dma((NX,)), dma, dma((NX,)), dma, dma((NX,)),
+                dma((2 * NX + 2,)), dma, dma((NX,)), dma, dma((NX,)), dma, dma((NX,)),
                 dma((4,)), dma((3, NX + 1)), dma((3,)), dma((3, 2, NX)),
                 dma((nf, 4)), dma((nf, KC)), dma((4, 8)), dma((4, 4)), dma((4, 2)),
                 dma, dma,

time: 78.7 us -> 78.7 us (level)
  no operation moved by 1% of the time
where the time goes in v6:
time: 78.7 us; the launch traced here: 78 us
  Pallas kernels  76.1 us (97%)
  local copies, waits for them, and re-layouts  1.87 us (2%)
    pallas_call x1, Pallas kernels, body(): pl.pallas_call(kernel, out_shape=jax.ShapeDtypeStruct((ROWS, W), BF), in_...  76.1 us
    unnamed x1, local copies, waits for them, and re-layouts  1.87 us

profile of v6, /device:TPU:2, one launch (start us, length us, event | category | flops | bytes accessed | tf_op | source)
XLA Modules:
  0.0 78.0 jit_solution(8804186171914744122)
XLA Ops:
  0.0 76.1 %shard_map.37 = bf16[1024,256]{1,0:T(8,128)(2,1)} custom-call(s32[64,64]{1,0:T(8,128)} %bitcast.3, bf16[8192,256]{1,0:T(8,128)(2,1)} %bitcast.2, bf16[8,2,128,128]{3,2,1,0:T(8,128)(2,1)} %inv_in.1), custom_call_target="tpu_custom_call" | custom-call | tf_op jit(solution)/shard_map/pallas_call | solution.py:537
  76.1 1.9 %copy.5 = bf16[1024,256]{1,0:T(8,128)(2,1)} copy(bf16[1024,256]{1,0:T(8,128)(2,1)} %shard_map.37) | data formatting | bytes 1048576
